TPU v7x, 32 devices: a whole 2x2x4 slice. The times are simulated.
32 devices in a mesh: seq: 4 (over y, x), dp: 8 (over z, core).
Axes of the slice: x: 2, y: 2, z: 4, core: 2. Of those that a mesh axis runs over, the one named last changes fastest.
Arguments:
- tokens: bfloat16 [8, 1024, 2048], P('dp', 'seq'), may hold values from -6 to 6
- cotangent: bfloat16 [8, 1024, 2048], P('dp', 'seq'), may hold values from -6 to 6
- first_gain: bfloat16 [2048], P(('seq', 'dp')), may hold values from 0.5 to 1.5
- first_shift: bfloat16 [2048], P(('seq', 'dp')), may hold values from -1.25 to 1.25
- second_gain: bfloat16 [2048], P(('seq', 'dp')), may hold values from 0.5 to 1.5
- second_shift: bfloat16 [2048], P(('seq', 'dp')), may hold values from -1.25 to 1.25
- joint_weight: bfloat16 [2048, 6144], P(('seq', 'dp')), may hold values from -0.125 to 0.125
- joint_bias: bfloat16 [6144], P(('seq', 'dp')), may hold values from -1.25 to 1.25
- dense_weight: bfloat16 [2048, 2048], P(('seq', 'dp')), may hold values from -1 to 1
- dense_bias: bfloat16 [2048], P(('seq', 'dp')), may hold values from -1.25 to 1.25
- expand_weight: bfloat16 [2048, 8192], P(('seq', 'dp')), may hold values from -0.125 to 0.125
- expand_bias: bfloat16 [8192], P(('seq', 'dp')), may hold values from -1.25 to 1.25
- shrink_weight: bfloat16 [8192, 2048], P(('seq', 'dp')), may hold values from -0.0625 to 0.0625
- shrink_bias: bfloat16 [2048], P(('seq', 'dp')), may hold values from -1.25 to 1.25
Outputs:
- output: bfloat16 [8, 1024, 2048], P('dp', 'seq')
- grad_tokens: float32 [8, 1024, 2048], P('dp', 'seq')
- grad_first_gain: float32 [2048], P(('seq', 'dp'))
- grad_first_shift: float32 [2048], P(('seq', 'dp'))
- grad_second_gain: float32 [2048], P(('seq', 'dp'))
- grad_second_shift: float32 [2048], P(('seq', 'dp'))
- grad_joint_weight: float32 [2048, 6144], P(('seq', 'dp'))
- grad_joint_bias: float32 [6144], P(('seq', 'dp'))
- grad_dense_weight: float32 [2048, 2048], P(('seq', 'dp'))
- grad_dense_bias: float32 [2048], P(('seq', 'dp'))
- grad_expand_weight: float32 [2048, 8192], P(('seq', 'dp'))
- grad_expand_bias: float32 [8192], P(('seq', 'dp'))
- grad_shrink_weight: float32 [8192, 2048], P(('seq', 'dp'))
- grad_shrink_bias: float32 [2048], P(('seq', 'dp'))
All inputs are finite; a program needn't handle non-finite values.
Results may differ from a plain program's by a relative error of at most 0.0089.
Values may be sent and summed in bfloat16 or wider, within the bound.
A program may use at most 384 MiB of HBM per device.

v0:
```python
import jax
import jax.numpy as jnp
from jax import lax
from jax.sharding import PartitionSpec as P

HEADS = 8
ROT = 64


def layer_norm(values, gain, shift):
    center = values - jnp.mean(values, axis=-1, keepdims=True)
    spread = jnp.mean(center * center, axis=-1, keepdims=True)
    return center * lax.rsqrt(spread + 1e-05) * gain + shift


def gelu_exact(values):
    return jax.nn.gelu(values, approximate=False)


def rotate(field, cosine, sine):
    half = ROT // 2
    part = field[..., :ROT]
    turned = jnp.concatenate([-part[..., half:], part[..., :half]], axis=-1)
    return jnp.concatenate([part * cosine + turned * sine, field[..., ROT:]], axis=-1)


def rotate_back(grad, cosine, sine):
    half = ROT // 2
    part = grad[..., :ROT]
    scaled = part * sine
    back = jnp.concatenate([scaled[..., half:], -scaled[..., :half]], axis=-1)
    return jnp.concatenate([part * cosine + back, grad[..., ROT:]], axis=-1)


def turn_tables(positions):
    inverse = 10000.0 ** (-jnp.arange(0, ROT, 2, dtype=jnp.float32) / ROT)
    angle = positions.astype(jnp.float32)[:, None] * inverse[None, :]
    angle = jnp.concatenate([angle, angle], axis=-1)[:, None, :]
    return (jnp.cos(angle), jnp.sin(angle))


def first_dims(left, right):
    return lax.dot_general(
        left, right, (((0,), (0,)), ((), ())), preferred_element_type=jnp.float32
    )


def last_dims(left, right):
    return lax.dot_general(
        left, right, (((1,), (1,)), ((), ())), preferred_element_type=jnp.float32
    )


def score_block(query_block, keys, first_row, scale):
    places = first_row + jnp.arange(query_block.shape[0], dtype=jnp.int32)
    key_places = jnp.arange(keys.shape[0], dtype=jnp.int32)
    visible = key_places[None, :] <= places[:, None]
    scores = (
        jnp.einsum("qhd,khd->hqk", query_block, keys, preferred_element_type=jnp.float32) * scale
    )
    return jnp.where(visible[None], scores, -1e30)


def attend_rows(query_block, first_row, keys, values, scale):
    scores = score_block(query_block, keys, first_row, scale)
    peak = jnp.max(scores, axis=-1, keepdims=True)
    expo = jnp.exp(scores - peak)
    total = jnp.sum(expo, axis=-1, keepdims=True)
    logsum = peak + jnp.log(total)
    probs_low = (expo / total).astype(jnp.bfloat16)
    mixed = jnp.einsum("hqk,khd->qhd", probs_low, values, preferred_element_type=jnp.float32)
    return (mixed.reshape(query_block.shape[0], -1).astype(jnp.bfloat16), logsum)


def attend_back(query_block, grad_mixed, logsum, first_row, keys, values, scale):
    scores = score_block(query_block, keys, first_row, scale)
    probs = jnp.exp(scores - logsum)
    grad_values_part = jnp.einsum(
        "hqk,qhd->khd", probs.astype(jnp.bfloat16), grad_mixed, preferred_element_type=jnp.float32
    )
    grad_probs = jnp.einsum("qhd,khd->hqk", grad_mixed, values, preferred_element_type=jnp.float32)
    inner = jnp.sum(probs * grad_probs, axis=-1, keepdims=True)
    grad_scores = (probs * (grad_probs - inner)).astype(jnp.bfloat16)
    grad_query = (
        jnp.einsum("hqk,khd->qhd", grad_scores, keys, preferred_element_type=jnp.float32) * scale
    )
    grad_keys_part = (
        jnp.einsum("hqk,qhd->khd", grad_scores, query_block, preferred_element_type=jnp.float32)
        * scale
    )
    return (grad_query, grad_keys_part, grad_values_part)


def fetch_all(shards):
    return (
        lax.all_gather(shards[0], ("seq", "dp"), axis=0, tiled=True),
        lax.all_gather(shards[1], ("seq", "dp"), axis=0, tiled=True),
        lax.all_gather(shards[2], ("seq", "dp"), axis=0, tiled=True),
        lax.all_gather(shards[3], ("seq", "dp"), axis=0, tiled=True),
        lax.all_gather(shards[4], ("seq", "dp"), axis=0, tiled=True),
        lax.all_gather(shards[5], ("seq", "dp"), axis=0, tiled=True),
        lax.all_gather(shards[6], ("seq", "dp"), axis=0, tiled=True),
        lax.all_gather(shards[7], ("seq", "dp"), axis=0, tiled=True),
        lax.all_gather(shards[8], ("seq", "dp"), axis=0, tiled=True),
        lax.all_gather(shards[9], ("seq", "dp"), axis=0, tiled=True),
        lax.all_gather(shards[10], ("seq", "dp"), axis=0, tiled=True),
        lax.all_gather(shards[11], ("seq", "dp"), axis=0, tiled=True),
    )


def reduce_all(grads):
    return (
        lax.psum_scatter(grads[0], ("seq", "dp"), scatter_dimension=0, tiled=True),
        lax.psum_scatter(grads[1], ("seq", "dp"), scatter_dimension=0, tiled=True),
        lax.psum_scatter(grads[2], ("seq", "dp"), scatter_dimension=0, tiled=True),
        lax.psum_scatter(grads[3], ("seq", "dp"), scatter_dimension=0, tiled=True),
        lax.psum_scatter(grads[4], ("seq", "dp"), scatter_dimension=0, tiled=True),
        lax.psum_scatter(grads[5], ("seq", "dp"), scatter_dimension=0, tiled=True),
    )


def sharded_plan(tokens, cotangent, shards):
    gathered = fetch_all(shards)
    (
        gain_one,
        shift_one,
        gain_two,
        shift_two,
        joint_full,
        joint_offset,
        dense_full,
        dense_offset,
        expand_full,
        expand_offset,
        shrink_full,
        shrink_offset,
    ) = gathered
    hidden = tokens[0].astype(jnp.float32)
    rows = hidden.shape[0]
    width = hidden.shape[1]
    head_size = width // HEADS
    normed_attn, pull_attn = jax.vjp(
        layer_norm, hidden, gain_one.astype(jnp.float32), shift_one.astype(jnp.float32)
    )
    normed_feed, pull_feed = jax.vjp(
        layer_norm, hidden, gain_two.astype(jnp.float32), shift_two.astype(jnp.float32)
    )
    normed_one = normed_attn.astype(jnp.bfloat16)
    normed_two = normed_feed.astype(jnp.bfloat16)
    joint = jnp.dot(
        normed_one, joint_full, preferred_element_type=jnp.float32
    ) + joint_offset.astype(jnp.float32)
    query = joint[:, :width].reshape(rows, HEADS, head_size)
    keyed = joint[:, width : 2 * width].reshape(rows, HEADS, head_size)
    valued = joint[:, 2 * width :].reshape(rows, HEADS, head_size)
    first_row = lax.axis_index("seq") * rows
    cosine, sine = turn_tables(first_row + jnp.arange(rows, dtype=jnp.int32))
    query_low = rotate(query, cosine, sine).astype(jnp.bfloat16)
    key_low = rotate(keyed, cosine, sine).astype(jnp.bfloat16)
    value_low = valued.astype(jnp.bfloat16)
    keys, values = (
        lax.all_gather(key_low, "seq", axis=0, tiled=True),
        lax.all_gather(value_low, "seq", axis=0, tiled=True),
    )
    scale = head_size ** (-0.5)
    mixed_low, logsum = attend_rows(query_low, first_row, keys, values, scale)
    attend = jnp.dot(
        mixed_low, dense_full, preferred_element_type=jnp.float32
    ) + dense_offset.astype(jnp.float32)
    pre = jnp.dot(
        normed_two, expand_full, preferred_element_type=jnp.float32
    ) + expand_offset.astype(jnp.float32)
    act, pull_gelu = jax.vjp(gelu_exact, pre)
    act_low = act.astype(jnp.bfloat16)
    feed = jnp.dot(act_low, shrink_full, preferred_element_type=jnp.float32) + shrink_offset.astype(
        jnp.float32
    )
    output = (hidden + attend + feed).astype(jnp.bfloat16)[None]
    gathered = fetch_all(lax.optimization_barrier((shards, output))[0])
    joint_full = gathered[4]
    dense_full = gathered[6]
    expand_full = gathered[8]
    shrink_full = gathered[10]
    upstream = cotangent[0]
    upstream_wide = upstream.astype(jnp.float32)
    upstream_total = jnp.sum(upstream_wide, axis=0)
    grad_shrink = first_dims(act_low, upstream)
    grad_act = last_dims(upstream, shrink_full)
    grad_pre = pull_gelu(grad_act)[0].astype(jnp.bfloat16)
    grad_expand = first_dims(normed_two, grad_pre)
    grad_expand_bias = jnp.sum(grad_pre.astype(jnp.float32), axis=0)
    grad_normed_two = last_dims(grad_pre, expand_full)
    grad_from_two, grad_gain_two, grad_shift_two = pull_feed(grad_normed_two)
    feed_grads = reduce_all(
        (grad_gain_two, grad_shift_two, grad_expand, grad_expand_bias, grad_shrink, upstream_total)
    )
    grad_dense = first_dims(mixed_low, upstream)
    grad_mixed = (
        last_dims(upstream, dense_full).astype(jnp.bfloat16).reshape(rows, HEADS, head_size)
    )
    grad_query, grad_keys_part, grad_values_part = attend_back(
        query_low, grad_mixed, logsum, first_row, keys, values, scale
    )
    grad_keyed, grad_valued = (
        lax.psum_scatter(grad_keys_part, "seq", scatter_dimension=0, tiled=True),
        lax.psum_scatter(grad_values_part, "seq", scatter_dimension=0, tiled=True),
    )
    grad_joint = jnp.concatenate(
        [
            rotate_back(grad_query, cosine, sine).reshape(rows, width),
            rotate_back(grad_keyed, cosine, sine).reshape(rows, width),
            grad_valued.reshape(rows, width),
        ],
        axis=1,
    ).astype(jnp.bfloat16)
    grad_joint_full = first_dims(normed_one, grad_joint)
    grad_joint_offset = jnp.sum(grad_joint.astype(jnp.float32), axis=0)
    grad_normed_one = last_dims(grad_joint, joint_full)
    grad_from_one, grad_gain_one, grad_shift_one = pull_attn(grad_normed_one)
    attend_grads = reduce_all(
        (
            grad_gain_one,
            grad_shift_one,
            grad_joint_full,
            grad_joint_offset,
            grad_dense,
            upstream_total,
        )
    )
    grad_tokens = (upstream_wide + grad_from_one + grad_from_two)[None]
    return (
        output,
        grad_tokens,
        attend_grads[0],
        attend_grads[1],
        feed_grads[0],
        feed_grads[1],
        attend_grads[2],
        attend_grads[3],
        attend_grads[4],
        attend_grads[5],
        feed_grads[2],
        feed_grads[3],
        feed_grads[4],
        feed_grads[5],
    )


def body(
    tokens,
    cotangent,
    first_gain,
    first_shift,
    second_gain,
    second_shift,
    joint_weight,
    joint_bias,
    dense_weight,
    dense_bias,
    expand_weight,
    expand_bias,
    shrink_weight,
    shrink_bias,
):
    shards = (
        first_gain,
        first_shift,
        second_gain,
        second_shift,
        joint_weight,
        joint_bias,
        dense_weight,
        dense_bias,
        expand_weight,
        expand_bias,
        shrink_weight,
        shrink_bias,
    )
    return sharded_plan(tokens, cotangent, shards)


def solution(mesh):
    return jax.shard_map(
        body,
        mesh=mesh,
        in_specs=(
            P("dp", "seq", None),
            P("dp", "seq", None),
            P(("seq", "dp")),
            P(("seq", "dp")),
            P(("seq", "dp")),
            P(("seq", "dp")),
            P(("seq", "dp"), None),
            P(("seq", "dp")),
            P(("seq", "dp"), None),
            P(("seq", "dp")),
            P(("seq", "dp"), None),
            P(("seq", "dp")),
            P(("seq", "dp"), None),
            P(("seq", "dp")),
        ),
        out_specs=(
            P("dp", "seq", None),
            P("dp", "seq", None),
            P(("seq", "dp")),
            P(("seq", "dp")),
            P(("seq", "dp")),
            P(("seq", "dp")),
            P(("seq", "dp"), None),
            P(("seq", "dp")),
            P(("seq", "dp"), None),
            P(("seq", "dp")),
            P(("seq", "dp"), None),
            P(("seq", "dp")),
            P(("seq", "dp"), None),
            P(("seq", "dp")),
        ),
        check_vma=False,
    )
```

profile of v0, /device:TPU:0, one launch (start us, length us, event | category | flops | bytes accessed | tf_op | source)
XLA Modules:
  0.0 3825.2 jit_solution(1538485691529107396)
XLA Ops:
  13.9 43.7 %all-reduce.15 = (bf16[6144]{0:T(1024)(128)(2,1)S(1)}, bf16[2048]{0:T(1024)(128)(2,1)S(1)}, bf16[2048]{0:T(1024)(128)(2,1)S(1)}, bf16[2048]{0:T(1024)(128)(2,1)S...) all-reduce(bf16[6144]{0:T(1024)(128)(2,1)S(1)} %dynamic-update-slic, ...), channel_id=1, replica_groups=mesh['seq'=4,'dp'=8] {'seq','dp'}, use_global_device_ids=true, to_apply=%add.2 | all-reduce | flops 18432 | bytes 73728
  61.6 108.3 %all-gather.12.cloned.1.call-done = bf16[2048,6144]{1,0:T(8,128)(2,1)} async-done(((bf16[64,6144]{1,0:T(8,128)(2,1)}), bf16[2048,6144]{1,0:T(8,128)(2,1)}) %all-gather.12.cloned.1.call-update) | async-done | bytes 25165840 | tf_op jit(solution)/shard_map/all_gather | solution.py:100
  195.7 38.9 %all-gather = bf16[32,1,256]{2,1,0:T(2,128)(2,1)S(1)} all-gather(bf16[1,1,256]{2,1,0:T(2,128)(2,1)S(1)} %reshape.225), channel_id=1, replica_groups=mesh['seq'=4,'dp'=8] {'seq','dp'}, dimensions={0}, use_global_device_ids=true | all-gather | bytes 16896 | tf_op jit(solution)/shard_map/all_gather | solution.py:105
  250.5 46.4 %all-gather.14.cloned.1.call-done = bf16[1024,8,256]{0,2,1:T(8,128)(2,1)} async-done(((bf16[256,8,256]{0,2,1:T(8,128)(2,1)}), bf16[1024,8,256]{0,2,1:T(8,128)(2,1)}) %all-gather.14.cloned.1.call-update) | async-done | bytes 4194320 | tf_op jit(solution)/shard_map/all_gather | solution.py:163
  303.4 73.8 %all-gather.18.cloned.1.call-done = bf16[2048,2048]{1,0:T(8,128)(2,1)} async-done(((bf16[64,2048]{1,0:T(8,128)(2,1)}), bf16[2048,2048]{1,0:T(8,128)(2,1)}) %all-gather.18.cloned.1.call-update) | async-done | bytes 8388624 | tf_op jit(solution)/shard_map/all_gather | solution.py:102
  384.2 189.2 %all-gather.20.cloned.1.call-done = bf16[2048,8192]{1,0:T(8,128)(2,1)} async-done(((bf16[64,8192]{1,0:T(8,128)(2,1)}), bf16[2048,8192]{1,0:T(8,128)(2,1)}) %all-gather.20.cloned.1.call-update) | async-done | bytes 33554448 | tf_op jit(solution)/shard_map/all_gather | solution.py:104
  573.4 18.2 convolution_add_fusion
  591.7 177.6 %all-gather.22.cloned.1.call-done = bf16[8192,2048]{1,0:T(8,128)(2,1)} async-done(((bf16[256,2048]{1,0:T(8,128)(2,1)}), bf16[8192,2048]{1,0:T(8,128)(2,1)}) %all-gather.22.cloned.1.call-update) | async-done | bytes 33554448 | tf_op jit(solution)/shard_map/all_gather | solution.py:106
  769.3 31.7 fusion.29
  801.5 75.1 %all-gather.24.cloned.1.call-done = bf16[2048,2048]{1,0:T(8,128)(2,1)} async-done(((bf16[64,2048]{1,0:T(8,128)(2,1)}), bf16[2048,2048]{1,0:T(8,128)(2,1)}) %all-gather.24.cloned.1.call-update) | async-done | bytes 8388624 | tf_op jit(solution)/shard_map/all_gather | solution.py:102
  914.0 69.6 %reduce-scatter.7.cloned.1.call-done = f32[256,8,256]{2,0,1:T(8,128)} async-done(((f32[1024,8,256]{2,0,1:T(8,128)}), f32[256,8,256]{2,0,1:T(8,128)}) %reduce-scatter.7.cloned.1.call-update) | async-done | bytes 2097168 | tf_op jit(solution)/shard_map/reduce_scatter | solution.py:205
  992.6 80.7 %reduce-scatter.9.cloned.1.call-done = f32[256,8,256]{0,2,1:T(8,128)} async-done(((f32[1024,8,256]{0,2,1:T(8,128)}), f32[256,8,256]{0,2,1:T(8,128)}) %reduce-scatter.9.cloned.1.call-update) | async-done | bytes 2097168 | tf_op jit(solution)/shard_map/reduce_scatter | solution.py:206
  1076.6 194.3 %all-gather.28.cloned.1.call-done = bf16[8192,2048]{1,0:T(8,128)(2,1)} async-done(((bf16[256,2048]{1,0:T(8,128)(2,1)}), bf16[8192,2048]{1,0:T(8,128)(2,1)}) %all-gather.28.cloned.1.call-update) | async-done | bytes 33554448 | tf_op jit(solution)/shard_map/all_gather | solution.py:106
  1271.0 33.7 convert_reduce_fusion
  1304.7 162.3 %all-gather.30.cloned.1.call-done = bf16[2048,8192]{1,0:T(8,128)(2,1)} async-done(((bf16[64,8192]{1,0:T(8,128)(2,1)}), bf16[2048,8192]{1,0:T(8,128)(2,1)}) %all-gather.30.cloned.1.call-update) | async-done | bytes 33554448 | tf_op jit(solution)/shard_map/all_gather | solution.py:104
  1484.7 138.1 %all-gather.26.cloned.1.call-done = bf16[2048,6144]{1,0:T(8,128)(2,1)} async-done(((bf16[64,6144]{1,0:T(8,128)(2,1)}), bf16[2048,6144]{1,0:T(8,128)(2,1)}) %all-gather.26.cloned.1.call-update) | async-done | bytes 25165840 | tf_op jit(solution)/shard_map/all_gather | solution.py:100
  1657.8 19.0 fusion.63
  1678.1 34.1 fusion.48
  1712.8 25.5 fusion.60
  1738.3 31.4 all-reduce.18.cloned.1.call-done
  1778.2 182.1 %reduce-scatter.13.cloned.1.call-done = f32[64,2048]{1,0:T(8,128)} async-done(((f32[2048,2048]{1,0:T(8,128)}), f32[64,2048]{1,0:T(8,128)}) %reduce-scatter.13.cloned.1.call-update) | async-done | bytes 524304 | tf_op jit(solution)/shard_map/reduce_scatter | solution.py:117
  1960.3 437.3 %reduce-scatter.11.cloned.1.call-done = f32[64,6144]{1,0:T(8,128)} async-done(((f32[2048,6144]{1,0:T(8,128)}), f32[64,6144]{1,0:T(8,128)}) %reduce-scatter.11.cloned.1.call-update) | async-done | bytes 1572880 | tf_op jit(solution)/shard_map/reduce_scatter | solution.py:115
  2397.6 711.3 %reduce-scatter.17.cloned.1.call-done = f32[256,2048]{1,0:T(8,128)} async-done(((f32[8192,2048]{1,0:T(8,128)}), f32[256,2048]{1,0:T(8,128)}) %reduce-scatter.17.cloned.1.call-update) | async-done | bytes 2097168 | tf_op jit(solution)/shard_map/reduce_scatter | solution.py:117
  3108.9 708.8 %reduce-scatter.15.cloned.1.call-done = f32[64,8192]{1,0:T(8,128)} async-done(((f32[2048,8192]{1,0:T(8,128)}), f32[64,8192]{1,0:T(8,128)}) %reduce-scatter.15.cloned.1.call-update) | async-done | bytes 2097168 | tf_op jit(solution)/shard_map/reduce_scatter | solution.py:115
  (196 shorter events, 178.9 us)
Async XLA Ops:
  7.2 162.7 %all-gather.12.cloned.1.call-start = ((), (), s32[]{:S(2)}) async-start(), calls=%async_computation.6 | async-start | bytes 25952256 | tf_op jit(solution)/shard_map/all_gather | solution.py:100
  7.9 234.0 %all-gather.16.cloned.1.call-start = ((), (), s32[]{:S(2)}) async-start(), calls=%async_computation.8 | async-start | bytes 5242880 | tf_op jit(solution)/shard_map/all_gather | solution.py:162
  59.9 513.5 %copy-start.24 = (f32[256]{0:T(256)}, f32[256]{0:T(256)S(1)}, u32[]{:S(2)}) copy-start(f32[256]{0:T(256)S(1)} %broadcast_multiply_fusion.1) | copy-start | bytes 3076
  61.6 511.8 %copy-start.26 = (f32[256]{0:T(256)}, f32[256]{0:T(256)S(1)}, u32[]{:S(2)}) copy-start(f32[256]{0:T(256)S(1)} %fusion.56) | copy-start | bytes 3076
  190.7 106.2 %all-gather.14.cloned.1.call-start = ((), (), s32[]{:S(2)}) async-start(), calls=%async_computation.7 | async-start | bytes 5242880 | tf_op jit(solution)/shard_map/all_gather | solution.py:163
  193.9 183.3 %all-gather.18.cloned.1.call-start = ((), (), s32[]{:S(2)}) async-start(), calls=%async_computation.9 | async-start | bytes 8650752 | tf_op jit(solution)/shard_map/all_gather | solution.py:102
  194.4 379.0 %all-gather.20.cloned.1.call-start = ((), (), s32[]{:S(2)}) async-start(), calls=%async_computation.10 | async-start | bytes 34603008 | tf_op jit(solution)/shard_map/all_gather | solution.py:104
  195.0 574.2 %all-gather.22.cloned.1.call-start = ((), (), s32[]{:S(2)}) async-start(), calls=%async_computation.11 | async-start | bytes 34603008 | tf_op jit(solution)/shard_map/all_gather | solution.py:106
  195.6 681.0 %all-gather.24.cloned.1.call-start = ((), (), s32[]{:S(2)}) async-start(), calls=%async_computation.12 | async-start | bytes 8650752 | tf_op jit(solution)/shard_map/all_gather | solution.py:102
  195.7 377.8 %copy-start.20 = (f32[2048]{0:T(1024)}, f32[2048]{0:T(1024)S(1)}, u32[]{:S(2)}) copy-start(f32[2048]{0:T(1024)S(1)} %convert_element_type.107) | copy-start | bytes 24580
  195.7 377.7 %copy-start.22 = (f32[2048]{0:T(1024)}, f32[2048]{0:T(1024)S(1)}, u32[]{:S(2)}) copy-start(f32[2048]{0:T(1024)S(1)} %convert_element_type.108) | copy-start | bytes 24580
  303.4 288.3 %copy-start.5 = (bf16[8,256,256]{2,1,0:T(8,128)(2,1)}, bf16[8,256,256]{2,1,0:T(8,128)(2,1)S(1)}, u32[]{:S(2)}) copy-start(bf16[8,256,256]{2,1,0:T(8,128)(2,1)S(1)} %fusion.41) | copy-start | bytes 3145732
  801.0 182.5 %reduce-scatter.7.cloned.1.call-start = ((), (), s32[]{:S(2)}) async-start(), calls=%async_computation.13 | async-start | bytes 10485760 | tf_op jit(solution)/shard_map/reduce_scatter | solution.py:205
  898.4 174.9 %reduce-scatter.9.cloned.1.call-start = ((), (), s32[]{:S(2)}) async-start(), calls=%async_computation.14 | async-start | bytes 10485760 | tf_op jit(solution)/shard_map/reduce_scatter | solution.py:206
  906.5 364.5 %all-gather.28.cloned.1.call-start = ((), (), s32[]{:S(2)}) async-start(), calls=%async_computation.16 | async-start | bytes 34603008 | tf_op jit(solution)/shard_map/all_gather | solution.py:106
  907.1 559.9 %all-gather.30.cloned.1.call-start = ((), (), s32[]{:S(2)}) async-start(), calls=%async_computation.17 | async-start | bytes 34603008 | tf_op jit(solution)/shard_map/all_gather | solution.py:104
  907.8 714.9 %all-gather.26.cloned.1.call-start = ((), (), s32[]{:S(2)}) async-start(), calls=%async_computation.15 | async-start | bytes 25952256 | tf_op jit(solution)/shard_map/all_gather | solution.py:100
  908.4 861.4 %all-reduce.18.cloned.1.call-start = ((), (), s32[]{:S(2)}) async-start(), calls=%async_computation.22 | async-start | bytes 196608
  992.6 312.1 %copy-start.4 = (bf16[256,8,256]{0,2,1:T(8,128)(2,1)}, bf16[256,8,256]{0,2,1:T(8,128)(2,1)S(1)}, u32[]{:S(2)}) copy-start(bf16[256,8,256]{0,2,1:T(8,128)(2,1)S(1)} %copy.96) | copy-start | bytes 3145732
  1647.5 312.8 %reduce-scatter.13.cloned.1.call-start = ((), (), s32[]{:S(2)}) async-start(), calls=%async_computation.19 | async-start | bytes 17301504 | tf_op jit(solution)/shard_map/reduce_scatter | solution.py:117
  1657.1 740.4 %reduce-scatter.11.cloned.1.call-start = ((), (), s32[]{:S(2)}) async-start(), calls=%async_computation.18 | async-start | bytes 51904512 | tf_op jit(solution)/shard_map/reduce_scatter | solution.py:115
  1676.9 1432.0 %reduce-scatter.17.cloned.1.call-start = ((), (), s32[]{:S(2)}) async-start(), calls=%async_computation.21 | async-start | bytes 69206016 | tf_op jit(solution)/shard_map/reduce_scatter | solution.py:117
  1712.2 2105.6 %reduce-scatter.15.cloned.1.call-start = ((), (), s32[]{:S(2)}) async-start(), calls=%async_computation.20 | async-start | bytes 69206016 | tf_op jit(solution)/shard_map/reduce_scatter | solution.py:115
  1770.5 2047.7 %copy-start.31 = (f32[64]{0:T(128)}, f32[64]{0:T(128)S(1)}, u32[]{:S(2)}) copy-start(f32[64]{0:T(128)S(1)} %dynamic-slice.5) | copy-start | bytes 772
  (27 other events, 2181.2 us)
Sparse Core Ops, SparseCore 0:
  11.0 158.8 all-gather.11
  190.9 51.0 all-gather.15
  244.3 52.5 all-gather.13
  299.7 77.3 all-gather.17
  380.0 193.3 all-gather.19
  576.3 192.9 all-gather.21
  801.2 75.4 all-gather.23
  898.5 84.9 reduce-scatter.6
  986.9 86.3 reduce-scatter.8
  1076.2 194.7 all-gather.27
  1274.0 192.9 all-gather.29
  1469.8 152.8 all-gather.25
  1647.6 122.1 all-reduce.17
  1772.6 187.6 reduce-scatter.12
  1968.3 429.2 reduce-scatter.10
  2400.5 708.3 reduce-scatter.16
  3111.8 705.8 reduce-scatter.14
where the time goes:
time: 3840 us; the launch traced here: 3830 us
  waiting for transfers between devices  3400 us (89%)
  matrix products  265 us (7%)
  blocking collectives  82.6 us (2%)
    reduce_scatter x2, waiting for transfers between devices, reduce_all(): lax.psum_scatter(grads[2], ('seq', 'dp'), scatter_dimension=0, tiled=True)  1150 us
    reduce_scatter x2, waiting for transfers between devices, reduce_all(): lax.psum_scatter(grads[4], ('seq', 'dp'), scatter_dimension=0, tiled=True)  893 us
    all_gather x2, waiting for transfers between devices, fetch_all(): lax.all_gather(shards[10], ('seq', 'dp'), axis=0, tiled=True)  372 us
    all_gather x2, waiting for transfers between devices, fetch_all(): lax.all_gather(shards[8], ('seq', 'dp'), axis=0, tiled=True)  351 us
    all_gather x2, waiting for transfers between devices, fetch_all(): lax.all_gather(shards[4], ('seq', 'dp'), axis=0, tiled=True)  246 us
    all_gather x2, waiting for transfers between devices, fetch_all(): lax.all_gather(shards[6], ('seq', 'dp'), axis=0, tiled=True)  149 us
    dot_general x4, matrix products, first_dims(): lax.dot_general(left, right, (((0,), (0,)), ((), ())), preferred_element_...  88.2 us
    reduce_scatter x1, waiting for transfers between devices, sharded_plan(): lax.psum_scatter(grad_values_part, 'seq', scatter_dimension=0, tiled=True)  80.7 us
  transfers between devices with their start and end apart: 17, of which 17 were waited for; matrix products, arithmetic and copies ran while one was open for 6% of the time, Pallas kernels for 0%

commit v1 on v0

v1 whole, which is shorter than its diff:
```python
import jax
import jax.numpy as jnp
from jax import lax
from jax.sharding import PartitionSpec as P

HEADS = 8
ROT = 64
CORES = 2
BF = jnp.bfloat16
F32 = jnp.float32


def mm(left, right):
    return jnp.dot(left, right, preferred_element_type=F32)


def mm_first(left, right):
    return lax.dot_general(left, right, (((0,), (0,)), ((), ())), preferred_element_type=F32)


def mm_last(left, right):
    return lax.dot_general(left, right, (((1,), (1,)), ((), ())), preferred_element_type=F32)


def rotate(field, cosine, sine):
    half = ROT // 2
    part = field[..., :ROT]
    turned = jnp.concatenate([-part[..., half:], part[..., :half]], axis=-1)
    return jnp.concatenate([part * cosine + turned * sine, field[..., ROT:]], axis=-1)


def rotate_back(grad, cosine, sine):
    half = ROT // 2
    part = grad[..., :ROT]
    scaled = part * sine
    back = jnp.concatenate([scaled[..., half:], -scaled[..., :half]], axis=-1)
    return jnp.concatenate([part * cosine + back, grad[..., ROT:]], axis=-1)


def turn_tables(length):
    inverse = 10000.0 ** (-jnp.arange(0, ROT, 2, dtype=F32) / ROT)
    angle = jnp.arange(length, dtype=F32)[:, None] * inverse[None, :]
    angle = jnp.concatenate([angle, angle], axis=-1)[:, None, :]
    return jnp.cos(angle), jnp.sin(angle)


class Ring:
    def __init__(self, n, m):
        self.n, self.m, self.line = n, m, m // CORES
        self.s = lax.axis_index("seq")
        self.d = lax.axis_index("dp")
        self.z, self.c = self.d // CORES, self.d % CORES
        self.up = [(i, i + CORES) for i in range(m - CORES)]
        self.down = [(i + CORES, i) for i in range(m - CORES)]
        self.swap = [(i, i ^ 1) for i in range(m)]

    def pick(self, stack, index):
        return lax.dynamic_index_in_dim(stack, index, 0, keepdims=False)

    def partner(self, k):
        return [(i, i ^ k) for i in range(self.n)]

    def order(self, slots):
        stack = jnp.stack(slots)
        return jnp.stack([self.pick(stack, self.s ^ j) for j in range(self.n)])

    def gather_seq(self, block):
        slots = [block] + [lax.ppermute(block, "seq", self.partner(k)) for k in range(1, self.n)]
        return self.order(slots)

    def exchange_seq(self, blocks):
        slots = [self.pick(blocks, self.s)]
        for k in range(1, self.n):
            slots.append(lax.ppermute(self.pick(blocks, self.s ^ k), "seq", self.partner(k)))
        return slots

    def scatter_seq(self, blocks):
        slots = self.exchange_seq(blocks)
        total = slots[0].astype(F32)
        for other in slots[1:]:
            total = total + other.astype(F32)
        return total

    def gather_dp(self, block):
        ups, downs = [block], [block]
        for _ in range(self.line - 1):
            ups.append(lax.ppermute(ups[-1], "dp", self.up))
            downs.append(lax.ppermute(downs[-1], "dp", self.down))
        span = jnp.stack(ups[::-1] + downs[1:])
        mine = lax.dynamic_slice_in_dim(span, self.line - 1 - self.z, self.line, 0)
        other = lax.ppermute(mine, "dp", self.swap)
        first = self.c == 0
        both = jnp.stack(
            [jnp.where(first, mine, other), jnp.where(first, other, mine)], axis=1
        )
        return both.reshape((self.m,) + block.shape)

    def scatter_dp(self, blocks):
        parts = blocks.reshape((self.line, CORES) + blocks.shape[1:])
        parts = jnp.swapaxes(parts, 0, 1)
        sent = lax.ppermute(self.pick(parts, 1 - self.c), "dp", self.swap)
        held = (self.pick(parts, self.c).astype(F32) + sent.astype(F32)).astype(BF)
        reach = self.line - 1
        rising, falling = None, None
        for i in range(1, self.line):
            first = self.pick(held, jnp.minimum(self.z + self.line - i, reach))
            second = self.pick(held, jnp.maximum(self.z - self.line + i, 0))
            if rising is not None:
                first = (first.astype(F32) + rising.astype(F32)).astype(BF)
                second = (second.astype(F32) + falling.astype(F32)).astype(BF)
            rising = lax.ppermute(first, "dp", self.up)
            falling = lax.ppermute(second, "dp", self.down)
        return self.pick(held, self.z).astype(F32) + rising.astype(F32) + falling.astype(F32)


def block_plan(n, m, tokens, cotangent, shards):
    (
        first_gain,
        first_shift,
        second_gain,
        second_shift,
        joint_weight,
        joint_bias,
        dense_weight,
        dense_bias,
        expand_weight,
        expand_bias,
        shrink_weight,
        shrink_bias,
    ) = shards
    ring = Ring(n, m)
    devices = n * m
    own, upstream = tokens[0], cotangent[0]
    rows, width = own.shape
    length = rows * n
    piece = width // devices
    head_size = width // HEADS
    heads = HEADS // n
    part = width // n
    hidden_part = expand_weight.shape[1] // n

    def shuffle(values):
        shape = values.shape[:-1]
        values = values.reshape(shape + (n, m, piece))
        return jnp.swapaxes(values, -3, -2).reshape(shape + (width,))

    def unshuffle(values):
        shape = values.shape[:-1]
        values = values.reshape(shape + (m, n, piece))
        return jnp.swapaxes(values, -3, -2).reshape(shape + (width,))

    vectors = (
        first_gain,
        first_shift,
        second_gain,
        second_shift,
        joint_bias,
        dense_bias,
        expand_bias,
        shrink_bias,
    )
    packed = lax.all_gather(jnp.concatenate(vectors)[None], ("seq", "dp"), axis=0, tiled=True)
    full, start = [], 0
    for vector in vectors:
        full.append(packed[:, start : start + vector.shape[0]].reshape(-1).astype(F32))
        start += vector.shape[0]
    gain_one, shift_one, gain_two, shift_two = [shuffle(v) for v in full[:4]]
    joint_offset, dense_offset, expand_offset, shrink_offset = full[4:]
    joint_offset = ring.pick(jnp.swapaxes(joint_offset.reshape(3, n, part), 0, 1), ring.s)
    joint_offset = joint_offset.reshape(3 * part)
    expand_offset = ring.pick(expand_offset.reshape(n, hidden_part), ring.s)

    all_tokens = ring.gather_seq(shuffle(own)).reshape(length, width)
    joint_blocks = jnp.transpose(joint_weight.reshape(piece, 3, n, part), (2, 0, 1, 3))
    joint_mine = ring.order(ring.exchange_seq(joint_blocks.reshape(n, piece, 3 * part)))
    expand_blocks = jnp.swapaxes(expand_weight.reshape(piece, n, hidden_part), 0, 1)
    expand_mine = ring.order(ring.exchange_seq(expand_blocks))
    all_upstream = ring.gather_seq(upstream).reshape(length, width)
    dense_full = ring.gather_dp(dense_weight).reshape(part, width)
    joint_full = ring.gather_dp(joint_mine).reshape(width, 3 * part)
    expand_full = ring.gather_dp(expand_mine).reshape(width, hidden_part)
    shrink_full = ring.gather_dp(shrink_weight).reshape(hidden_part, width)

    values = all_tokens.astype(F32)
    center = values - jnp.mean(values, axis=-1, keepdims=True)
    spread = lax.rsqrt(jnp.mean(center * center, axis=-1, keepdims=True) + 1e-05)
    normal = center * spread
    normed_one = (normal * gain_one + shift_one).astype(BF)
    normed_two = (normal * gain_two + shift_two).astype(BF)

    joint = mm(normed_one, joint_full) + joint_offset
    query, keyed, valued = [
        joint[:, i * part : (i + 1) * part].reshape(length, heads, head_size) for i in range(3)
    ]
    cosine, sine = turn_tables(length)
    query = rotate(query, cosine, sine).astype(BF)
    keyed = rotate(keyed, cosine, sine).astype(BF)
    valued = valued.astype(BF)
    scale = head_size ** (-0.5)
    places = jnp.arange(length, dtype=jnp.int32)
    visible = places[None, :] <= places[:, None]
    scores = jnp.einsum("qhd,khd->hqk", query, keyed, preferred_element_type=F32) * scale
    scores = jnp.where(visible[None], scores, -1e30)
    peak = jnp.max(scores, axis=-1, keepdims=True)
    expo = jnp.exp(scores - peak)
    probs = expo / jnp.sum(expo, axis=-1, keepdims=True)
    probs_low = probs.astype(BF)
    mixed = jnp.einsum("hqk,khd->qhd", probs_low, valued, preferred_element_type=F32)
    mixed = mixed.reshape(length, part).astype(BF)

    grad_dense = mm_first(mixed, all_upstream).astype(BF)
    grad_mixed = mm_last(all_upstream, dense_full).astype(BF).reshape(length, heads, head_size)
    grad_valued = jnp.einsum("hqk,qhd->khd", probs_low, grad_mixed, preferred_element_type=F32)
    grad_probs = jnp.einsum("qhd,khd->hqk", grad_mixed, valued, preferred_element_type=F32)
    inner = jnp.sum(probs * grad_probs, axis=-1, keepdims=True)
    grad_scores = (probs * (grad_probs - inner)).astype(BF)
    grad_query = jnp.einsum("hqk,khd->qhd", grad_scores, keyed, preferred_element_type=F32) * scale
    grad_keyed = jnp.einsum("hqk,qhd->khd", grad_scores, query, preferred_element_type=F32) * scale
    grad_joint = jnp.concatenate(
        [
            rotate_back(grad_query, cosine, sine).reshape(length, part),
            rotate_back(grad_keyed, cosine, sine).reshape(length, part),
            grad_valued.reshape(length, part),
        ],
        axis=1,
    ).astype(BF)
    grad_joint_weight = mm_first(normed_one, grad_joint).astype(BF)
    grad_joint_offset = jnp.sum(grad_joint.astype(F32), axis=0)
    grad_normed_one = mm_last(grad_joint, joint_full)

    pre = mm(normed_two, expand_full) + expand_offset
    act, pull_gelu = jax.vjp(lambda v: jax.nn.gelu(v, approximate=False), pre)
    act = act.astype(BF)
    grad_shrink = mm_first(act, all_upstream).astype(BF)
    grad_pre = pull_gelu(mm_last(all_upstream, shrink_full))[0].astype(BF)
    grad_expand = mm_first(normed_two, grad_pre).astype(BF)
    grad_expand_offset = jnp.sum(grad_pre.astype(F32), axis=0)
    grad_normed_two = mm_last(grad_pre, expand_full)

    partial = (mm(mixed, dense_full) + mm(act, shrink_full)).astype(BF)
    summed = ring.scatter_seq(partial.reshape(n, rows, width))
    own_wide = own.astype(F32)
    output = (own_wide + (summed + (dense_offset + shrink_offset))).astype(BF)[None]

    grad_normal = (grad_normed_one * gain_one + grad_normed_two * gain_two).astype(BF)
    grad_normal = unshuffle(ring.scatter_seq(grad_normal.reshape(n, rows, width)))
    own_center = own_wide - jnp.mean(own_wide, axis=-1, keepdims=True)
    own_spread = lax.rsqrt(jnp.mean(own_center * own_center, axis=-1, keepdims=True) + 1e-05)
    own_normal = own_center * own_spread
    through = grad_normal - jnp.mean(grad_normal, axis=-1, keepdims=True)
    through = through - own_normal * jnp.mean(grad_normal * own_normal, axis=-1, keepdims=True)
    upstream_wide = upstream.astype(F32)
    grad_tokens = (upstream_wide + own_spread * through)[None]

    def placed(vector, groups):
        blocks = vector.reshape(groups, 1, -1)
        mine = (jnp.arange(n) == ring.s).reshape(1, n, 1)
        return jnp.where(mine, blocks, 0.0).reshape(-1)

    sums = (
        unshuffle(jnp.sum(grad_normed_one * normal, axis=0)),
        unshuffle(jnp.sum(grad_normed_one, axis=0)),
        unshuffle(jnp.sum(grad_normed_two * normal, axis=0)),
        unshuffle(jnp.sum(grad_normed_two, axis=0)),
        placed(grad_joint_offset, 3),
        placed(grad_expand_offset, 1),
        jnp.sum(upstream_wide, axis=0),
    )
    sums = jnp.concatenate([v.reshape(devices, -1) for v in sums], axis=1)
    sums = lax.psum_scatter(sums, ("seq", "dp"), scatter_dimension=0, tiled=True)[0]
    small, start = [], 0
    for length_of in (piece, piece, piece, piece, joint_bias.shape[0], expand_bias.shape[0], piece):
        small.append(sums[start : start + length_of])
        start += length_of

    def by_rows(grad):
        return ring.scatter_dp(grad.reshape((m, -1) + grad.shape[1:]))

    dense_grad = by_rows(grad_dense)
    joint_grad = by_rows(grad_joint_weight).astype(BF).reshape(n, piece, 3, part)
    shrink_grad = by_rows(grad_shrink)
    expand_grad = by_rows(grad_expand).astype(BF).reshape(n, piece, hidden_part)
    joint_grad = ring.order(ring.exchange_seq(joint_grad))
    joint_grad = jnp.transpose(joint_grad, (1, 2, 0, 3)).reshape(piece, 3 * width).astype(F32)
    expand_grad = ring.order(ring.exchange_seq(expand_grad))
    expand_grad = jnp.swapaxes(expand_grad, 0, 1).reshape(piece, n * hidden_part).astype(F32)
    return (
        output,
        grad_tokens,
        small[0],
        small[1],
        small[2],
        small[3],
        joint_grad,
        small[4],
        dense_grad,
        small[6],
        expand_grad,
        small[5],
        shrink_grad,
        small[6],
    )


def solution(mesh):
    n, m = mesh.shape["seq"], mesh.shape["dp"]

    def body(tokens, cotangent, *shards):
        return block_plan(n, m, tokens, cotangent, shards)

    both = ("seq", "dp")
    tokens = P("dp", "seq", None)
    vector, matrix = P(both), P(both, None)
    return jax.shard_map(
        body,
        mesh=mesh,
        in_specs=(tokens, tokens) + (vector,) * 4 + (matrix, vector) * 4,
        out_specs=(tokens, tokens) + (vector,) * 4 + (matrix, vector) * 4,
        check_vma=False,
    )
```

time: 3840 us -> 1100 us (0.29)
  waiting for transfers between devices: 3400 us -> 409 us
  starting transfers between devices: 1.09 us -> 167 us
  local copies, waits for them, and re-layouts: 34.8 us -> 173 us
  matrix products: 265 us -> 169 us
  other arithmetic: 29.8 us -> 112 us
  blocking collectives: 82.6 us -> 43.7 us
    reduce_scatter x6 -> x0, waiting for transfers between devices: 2190 us -> none  [the longest x2 1150 us: reduce_all(): lax.psum_scatter(grads[2], ('seq', 'dp'), scatter_dimension=0, tiled=True)]
    all_gather x10 -> x0, waiting for transfers between devices: 1170 us -> none  [the longest x2 372 us: fetch_all(): lax.all_gather(shards[10], ('seq', 'dp'), axis=0, tiled=True)]
    ppermute x0 -> x80, waiting for transfers between devices: none -> 284 us  [the longest x12 88.2 us: gather_dp(): downs.append(lax.ppermute(downs[-1], 'dp', self.down))]
    ppermute x0 -> x80, starting transfers between devices: none -> 167 us  [the longest x12 56.5 us: scatter_dp(): rising = lax.ppermute(first, 'dp', self.up)]
    dot_general x18 -> x17, matrix products: 265 us -> 160 us  [the longest x4 64.4 us: mm_last(): lax.dot_general(left, right, (((1,), (1,)), ((), ())), preferred_element_...]
    unnamed x18 -> x2, waiting for transfers between devices: 35.6 us -> 125 us
    convert_element_type x10 -> x25, other arithmetic: 1.76 us -> 53.8 us  [the longest x4 13.7 us: scatter_dp(): held = (self.pick(parts, self.c).astype(F32) + sent.astype(F32)).astype(BF)]
    all_gather x1 -> x0, blocking collectives: 38.9 us -> none  [fetch_all(): lax.all_gather(shards[9], ('seq', 'dp'), axis=0, tiled=True)]
  transfers between devices with their start and end apart: 17 -> 81, of which waited for: 17 -> 29; matrix products, arithmetic and copies ran while one was open for 6% -> 40% of each run, Pallas kernels for 0% -> 0%
where the time goes in v1:
time: 1100 us; the launch traced here: 1090 us
  waiting for transfers between devices  409 us (37%)
  local copies, waits for them, and re-layouts  173 us (16%)
  matrix products  169 us (15%)
  starting transfers between devices  167 us (15%)
  other arithmetic  112 us (10%)
  blocking collectives  43.7 us (4%)
  between operations  16.9 us (2%)
    unnamed x2, waiting for transfers between devices  125 us
    ppermute x12, waiting for transfers between devices, gather_dp(): downs.append(lax.ppermute(downs[-1], 'dp', self.down))  88.2 us
    ppermute x12, waiting for transfers between devices, scatter_dp(): rising = lax.ppermute(first, 'dp', self.up)  84.3 us
    dot_general x4, matrix products, mm_last(): lax.dot_general(left, right, (((1,), (1,)), ((), ())), preferred_element_...  64.4 us
    ppermute x12, starting transfers between devices, scatter_dp(): rising = lax.ppermute(first, 'dp', self.up)  56.5 us
    ppermute x12, starting transfers between devices, gather_dp(): ups.append(lax.ppermute(ups[-1], 'dp', self.up))  48.1 us
    unnamed x233, local copies, waits for them, and re-layouts  46.7 us
    unnamed x1, blocking collectives  43.7 us
  transfers between devices with their start and end apart: 81, of which 29 were waited for; matrix products, arithmetic and copies ran while one was open for 40% of the time, Pallas kernels for 0%

profile of v1, /device:TPU:0, one launch (start us, length us, event | category | flops | bytes accessed | tf_op | source)
XLA Modules:
  0.0 1090.7 jit_solution(10925251507789823282)
XLA Ops:
  23.1 43.7 %all-reduce = bf16[26624]{0:T(1024)(128)(2,1)S(1)} all-reduce(bf16[26624]{0:T(1024)(128)(2,1)S(1)} %dynamic-update-slice), channel_id=2, replica_groups=mesh['seq'=4,'dp'=8] {'seq','dp'}, use_global_device_ids=true, to_apply=%add | all-reduce | flops 26624 | bytes 106496
  130.2 22.5 %collective-permute-done.1 = bf16[256,2048]{0,1:T(8,128)(2,1)S(1)} collective-permute-done((bf16[256,2048]{0,1:T(8,128)(2,1)S(1)}, bf16[256,2048]{0,1:T(8,128)(2,1)S(1)}, u32[]{:S(2)}, u32[]{:S(2)}) %collective-permute-start.1) | collective-permute-done | bytes 1048608 | tf_op jit(solution)/shard_map/ppermute | solution.py:68
  161.1 14.9 %collective-permute-done.6 = bf16[4,64,1536]{2,1,0:T(8,128)(2,1)} collective-permute-done((bf16[4,64,1536]{2,1,0:T(8,128)(2,1)S(1)}, bf16[4,64,1536]{2,1,0:T(8,128)(2,1)}, u32[]{:S(2)}, u32[]{:S(2)}) %collective-permute-start.6) | collective-permute-done | bytes 786464 | tf_op jit(solution)/shard_map/ppermute | solution.py:87
  182.1 16.8 %collective-permute-done.9 = bf16[4,64,1536]{2,1,0:T(8,128)(2,1)S(1)} collective-permute-done((bf16[4,64,1536]{2,1,0:T(8,128)(2,1)S(1)}, bf16[4,64,1536]{2,1,0:T(8,128)(2,1)S(1)}, u32[]{:S(2)}, u32[]{:S(2)}) %collective-permute-start.9) | collective-permute-done | bytes 786464 | tf_op jit(solution)/shard_map/ppermute | solution.py:88
  276.0 12.7 %collective-permute-done.34 = bf16[256,2048]{1,0:T(8,128)(2,1)S(1)} collective-permute-done((bf16[256,2048]{1,0:T(8,128)(2,1)}, bf16[256,2048]{1,0:T(8,128)(2,1)S(1)}, u32[]{:S(2)}, u32[]{:S(2)}) %collective-permute-start.34) | collective-permute-done | bytes 1048608 | tf_op jit(solution)/shard_map/ppermute | solution.py:88
  298.5 12.6 %collective-permute-done.27 = bf16[4,64,2048]{2,1,0:T(8,128)(2,1)S(1)} collective-permute-done((bf16[4,64,2048]{2,1,0:T(8,128)(2,1)}, bf16[4,64,2048]{2,1,0:T(8,128)(2,1)S(1)}, u32[]{:S(2)}, u32[]{:S(2)}) %collective-permute-start.27) | collective-permute-done | bytes 1048608 | tf_op jit(solution)/shard_map/ppermute | solution.py:88
  339.4 11.1 %collective-permute-done.35 = bf16[256,2048]{1,0:T(8,128)(2,1)S(1)} collective-permute-done((bf16[256,2048]{1,0:T(8,128)(2,1)S(1)}, bf16[256,2048]{1,0:T(8,128)(2,1)S(1)}, u32[]{:S(2)}, u32[]{:S(2)}) %collective-permute-start.35) | collective-permute-done | bytes 1048608 | tf_op jit(solution)/shard_map/ppermute | solution.py:88
  360.9 11.3 %collective-permute-done.28 = bf16[4,64,2048]{2,1,0:T(8,128)(2,1)S(1)} collective-permute-done((bf16[4,64,2048]{2,1,0:T(8,128)(2,1)S(1)}, bf16[4,64,2048]{2,1,0:T(8,128)(2,1)S(1)}, u32[]{:S(2)}, u32[]{:S(2)}) %collective-permute-start.28) | collective-permute-done | bytes 1048608 | tf_op jit(solution)/shard_map/ppermute | solution.py:88
  526.4 12.6 %fusion.97 = f32[1024,2048]{1,0:T(8,128)S(1)} fusion(bf16[1024,2048]{1,0:T(8,128)(2,1)} %bitcast.463, bf16[2048,2048]{1,0:T(8,128)(2,1)} %bitcast.440), kind=kOutput, calls=%fused_computation.339 | convolution fusion | flops 8589934592 | bytes 20971520 | tf_op jit(solution)/shard_map/dot_general | solution.py:14
  539.1 29.3 %convert_reduce_fusion = (f32[2048]{0:T(1024)S(1)}, bf16[1024,2048]{1,0:T(8,128)(2,1)}, f32[1024,2048]{1,0:T(8,128)}) fusion(f32[1024,2048]{1,0:T(8,128)S(1)} %fusion.97, f32[2048]{0:T(1024)S(1)} %bitcast.506, bf16[1024,2048]{1,0:T(8,128)(2,1)S(1)} %bitcast.462, bf16[2048,2048]{1,0:T(8,128)(2,1)S(1)} %bitcast.437), kind=kOutput, calls=%fused_computation.13 | convolution fusion | flops 8747218944 | bytes 33570816 | tf_op jit(solution)/shard_map/dot_general | solution.py:22
  568.5 10.0 multiply_convert_fusion.1
  578.5 22.4 %multiply_reduce_fusion = (f32[2048]{0:T(1024)S(1)}, f32[2048]{0:T(1024)S(1)}, f32[2048]{0:T(1024)S(1)}, f32[2048]{0:T(1024)S(1)}, bf16[1024,2048]{1,0:T(8,128)(...) fusion(f32[4,256,2048]{2,1,0:T(8,128)} %copy.213, f32[1024]{0:T(1024)S(1)} %bitcast.508, ...), kind=kOutput, calls=%fused_computation.14 | convolution fusion | flops 8627675136 | bytes 42016768 | tf_op jit(solution)/shard_map/dot_general | solution.py:22
  600.9 12.0 %convolution_convert_fusion.1 = bf16[2048,2048]{1,0:T(8,128)(2,1)S(1)} fusion(bf16[1024,2048]{1,0:T(8,128)(2,1)} %get-tuple-element.66, bf16[1024,2048]{1,0:T(8,128)(2,1)} %get-tuple-element.61), kind=kOutput, calls=%fused_computation.41 | convolution fusion | flops 8594128896 | bytes 16777216 | tf_op jit(solution)/shard_map/dot_general | solution.py:18
  620.5 10.0 convolution_convert_fusion.2
  635.2 13.8 %add_convert_fusion.4 = bf16[1024,2048]{1,0:T(8,128)(2,1)S(1)} fusion(f32[1024,2048]{1,0:T(8,128)} %fusion.96, bf16[1024,2048]{1,0:T(8,128)(2,1)} %multiply_convert_fusion.1, bf16[2048,2048]{1,0:T(8,128)(2,1)} %bitcast.434), kind=kOutput, calls=%fused_computation.20 | convolution fusion | flops 8594128896 | bytes 25165824 | tf_op jit(solution)/shard_map/dot_general | solution.py:14
  656.3 14.1 %convolution_convert_fusion = bf16[2048,2048]{1,0:T(8,128)(2,1)} fusion(bf16[1024,2048]{1,0:T(8,128)(2,1)} %multiply_convert_fusion.1, bf16[1024,2048]{1,0:T(8,128)(2,1)} %bitcast.461), kind=kOutput, calls=%fused_computation.40 | convolution fusion | flops 8594128896 | bytes 16777216 | tf_op jit(solution)/shard_map/dot_general | solution.py:18
  690.0 125.4 %all-reduce.4.cloned.1.call-done = f32[32,768]{1,0:T(8,128)} async-done(((f32[32,768]{1,0:T(8,128)}), f32[32,768]{1,0:T(8,128)}) %all-reduce.4.cloned.1.call-update) | async-done | bytes 98320
  833.5 14.1 %collective-permute-done.43 = bf16[256,2048]{0,1:T(8,128)(2,1)S(1)} collective-permute-done((bf16[256,2048]{0,1:T(8,128)(2,1)}, bf16[256,2048]{0,1:T(8,128)(2,1)S(1)}, u32[]{:S(2)}, u32[]{:S(2)}) %collective-permute-start.43) | collective-permute-done | bytes 1048608 | tf_op jit(solution)/shard_map/ppermute | solution.py:74
  852.8 18.1 %collective-permute-done.44 = bf16[256,2048]{0,1:T(8,128)(2,1)S(1)} collective-permute-done((bf16[256,2048]{0,1:T(8,128)(2,1)}, bf16[256,2048]{0,1:T(8,128)(2,1)S(1)}, u32[]{:S(2)}, u32[]{:S(2)}) %collective-permute-start.44) | collective-permute-done | bytes 1048608 | tf_op jit(solution)/shard_map/ppermute | solution.py:74
  902.3 18.5 %collective-permute-done.64 = bf16[256,2048]{1,0:T(8,128)(2,1)S(1)} collective-permute-done((bf16[256,2048]{1,0:T(8,128)(2,1)S(1)}, bf16[256,2048]{1,0:T(8,128)(2,1)S(1)}, u32[]{:S(2)}, u32[]{:S(2)}) %collective-permute-start.64) | collective-permute-done | bytes 1048608 | tf_op jit(solution)/shard_map/ppermute | solution.py:111
  927.2 16.1 %collective-permute-done.74 = bf16[256,2048]{1,0:T(8,128)(2,1)S(1)} collective-permute-done((bf16[256,2048]{1,0:T(8,128)(2,1)S(1)}, bf16[256,2048]{1,0:T(8,128)(2,1)S(1)}, u32[]{:S(2)}, u32[]{:S(2)}) %collective-permute-start.74) | collective-permute-done | bytes 1048608 | tf_op jit(solution)/shard_map/ppermute | solution.py:111
  953.6 12.2 %collective-permute-done.65 = bf16[256,2048]{1,0:T(8,128)(2,1)S(1)} collective-permute-done((bf16[256,2048]{1,0:T(8,128)(2,1)S(1)}, bf16[256,2048]{1,0:T(8,128)(2,1)S(1)}, u32[]{:S(2)}, u32[]{:S(2)}) %collective-permute-start.65) | collective-permute-done | bytes 1048608 | tf_op jit(solution)/shard_map/ppermute | solution.py:111
  969.2 34.4 %collective-permute-done.75 = bf16[256,2048]{1,0:T(8,128)(2,1)S(1)} collective-permute-done((bf16[256,2048]{1,0:T(8,128)(2,1)S(1)}, bf16[256,2048]{1,0:T(8,128)(2,1)S(1)}, u32[]{:S(2)}, u32[]{:S(2)}) %collective-permute-start.75) | collective-permute-done | bytes 1048608 | tf_op jit(solution)/shard_map/ppermute | solution.py:111
  1063.0 14.2 %collective-permute-done.79 = bf16[256,2048]{1,0:T(8,128)(2,1)} collective-permute-done((bf16[256,2048]{1,0:T(8,128)(2,1)S(1)}, bf16[256,2048]{1,0:T(8,128)(2,1)}, u32[]{:S(2)}, u32[]{:S(2)}) %collective-permute-start.79) | collective-permute-done | bytes 1048608 | tf_op jit(solution)/shard_map/ppermute | solution.py:112
  (577 shorter events, 550.8 us)
Async XLA Ops:
  7.3 808.1 %all-reduce.4.cloned.1.call-start = ((), (), s32[]{:S(2)}) async-start(), calls=%async_computation | async-start | bytes 196608
  7.3 87.9 %collective-permute-start.13 = (bf16[64,2048]{1,0:T(8,128)(2,1)}, bf16[64,2048]{1,0:T(8,128)(2,1)}, u32[]{:S(2)}, u32[]{:S(2)}) collective-permute-start(bf16[64,2048]{1,0:T(8,128)(2,1)} %param.22), channel_id=1, source_target_pairs={{0,2},{1,3},{2,4},{3,5},{4,6},{5,7},{8,10},{9,11},{10,12},{11,13},... | collective-permute-start | bytes 786440 | tf_op jit(solution)/shard_map/ppermute | solution.py:87
  13.1 95.1 %collective-permute-start.16 = (bf16[64,2048]{1,0:T(8,128)(2,1)}, bf16[64,2048]{1,0:T(8,128)(2,1)}, u32[]{:S(2)}, u32[]{:S(2)}) collective-permute-start(bf16[64,2048]{1,0:T(8,128)(2,1)} %param.22), channel_id=1, source_target_pairs={{2,0},{3,1},{4,2},{5,3},{6,4},{7,5},{10,8},{11,9},{12,10},{13,11},... | collective-permute-start | bytes 786440 | tf_op jit(solution)/shard_map/ppermute | solution.py:88
  19.2 70.7 %collective-permute-start.3 = (bf16[64,1536]{1,0:T(8,128)(2,1)}, bf16[64,1536]{1,0:T(8,128)(2,1)}, u32[]{:S(2)}, u32[]{:S(2)}) collective-permute-start(bf16[64,1536]{1,0:T(8,128)(2,1)} %get-tuple-element.155), channel_id=1, source_target_pairs={{0,8},{8,0},{16,24},{24,16},{1,9},{9,1},{17,25},{25,17},{2,10},{10... | collective-permute-start | bytes 589832 | tf_op jit(solution)/shard_map/ppermute | solution.py:74
  20.7 71.5 %collective-permute-start.4 = (bf16[64,1536]{1,0:T(8,128)(2,1)}, bf16[64,1536]{1,0:T(8,128)(2,1)}, u32[]{:S(2)}, u32[]{:S(2)}) collective-permute-start(bf16[64,1536]{1,0:T(8,128)(2,1)} %get-tuple-element.154), channel_id=1, source_target_pairs={{0,16},{8,24},{16,0},{24,8},{1,17},{9,25},{17,1},{25,9},{2,18},{10... | collective-permute-start | bytes 589832 | tf_op jit(solution)/shard_map/ppermute | solution.py:74
  22.2 70.5 %collective-permute-start.5 = (bf16[64,1536]{1,0:T(8,128)(2,1)}, bf16[64,1536]{1,0:T(8,128)(2,1)}, u32[]{:S(2)}, u32[]{:S(2)}) collective-permute-start(bf16[64,1536]{1,0:T(8,128)(2,1)} %get-tuple-element.153), channel_id=1, source_target_pairs={{0,24},{8,16},{16,8},{24,0},{1,25},{9,17},{17,9},{25,1},{2,26},{10... | collective-permute-start | bytes 589832 | tf_op jit(solution)/shard_map/ppermute | solution.py:74
  117.3 92.2 %collective-permute-start.40 = (bf16[256,2048]{1,0:T(8,128)(2,1)S(1)}, bf16[256,2048]{1,0:T(8,128)(2,1)S(1)}, u32[]{:S(2)}, u32[]{:S(2)}) collective-permute-start(bf16[256,2048]{1,0:T(8,128)(2,1)S(1)} %bitcast.427), channel_id=1, source_target_pairs={{0,8},{8,0},{16,24},{24,16},{1,9},{9,1},{17,25},{25,17},{2,10},{10... | collective-permute-start | bytes 3145736 | tf_op jit(solution)/shard_map/ppermute | solution.py:68
  126.8 84.0 %collective-permute-start.41 = (bf16[256,2048]{1,0:T(8,128)(2,1)S(1)}, bf16[256,2048]{1,0:T(8,128)(2,1)S(1)}, u32[]{:S(2)}, u32[]{:S(2)}) collective-permute-start(bf16[256,2048]{1,0:T(8,128)(2,1)S(1)} %bitcast.428), channel_id=1, source_target_pairs={{0,16},{8,24},{16,0},{24,8},{1,17},{9,25},{17,1},{25,9},{2,18},{10... | collective-permute-start | bytes 3145736 | tf_op jit(solution)/shard_map/ppermute | solution.py:68
  128.6 82.3 %collective-permute-start.42 = (bf16[256,2048]{1,0:T(8,128)(2,1)S(1)}, bf16[256,2048]{1,0:T(8,128)(2,1)S(1)}, u32[]{:S(2)}, u32[]{:S(2)}) collective-permute-start(bf16[256,2048]{1,0:T(8,128)(2,1)S(1)} %bitcast.429), channel_id=1, source_target_pairs={{0,24},{8,16},{16,8},{24,0},{1,25},{9,17},{17,9},{25,1},{2,26},{10... | collective-permute-start | bytes 3145736 | tf_op jit(solution)/shard_map/ppermute | solution.py:68
  314.5 57.8 %collective-permute-start.28 = (bf16[4,64,2048]{2,1,0:T(8,128)(2,1)S(1)}, bf16[4,64,2048]{2,1,0:T(8,128)(2,1)S(1)}, u32[]{:S(2)}, u32[]{:S(2)}) collective-permute-start(bf16[4,64,2048]{2,1,0:T(8,128)(2,1)S(1)} %collective-permute-done.27), channel_id=1, source_target_pairs={{2,0},{3,1},{4,2},{5,3},{6,4},{7,5},{10,8},{11,9},{12,10},{13,11},... | collective-permute-start | bytes 3145736 | tf_op jit(solution)/shard_map/ppermute | solution.py:88
  354.9 139.0 %collective-permute-start.36 = (bf16[4,256,2048]{2,1,0:T(8,128)(2,1)}, bf16[4,256,2048]{2,1,0:T(8,128)(2,1)}, u32[]{:S(2)}, u32[]{:S(2)}) collective-permute-start(bf16[4,256,2048]{2,1,0:T(8,128)(2,1)} %constant_dynamic-slice_fusion.25), channel_id=1, source_target_pairs={{0,1},{1,0},{2,3},{3,2},{4,5},{5,4},{6,7},{7,6},{8,9},{9,8},{10,11... | collective-permute-start | bytes 12582920 | tf_op jit(solution)/shard_map/ppermute | solution.py:91
  376.5 129.7 %collective-permute-start.29 = (bf16[4,4,64,2048]{3,2,1,0:T(8,128)(2,1)}, bf16[4,4,64,2048]{3,2,1,0:T(8,128)(2,1)}, u32[]{:S(2)}, u32[]{:S(2)}) collective-permute-start(bf16[4,4,64,2048]{3,2,1,0:T(8,128)(2,1)} %constant_dynamic-slice_fusion.27), channel_id=1, source_target_pairs={{0,1},{1,0},{2,3},{3,2},{4,5},{5,4},{6,7},{7,6},{8,9},{9,8},{10,11... | collective-permute-start | bytes 12582920 | tf_op jit(solution)/shard_map/ppermute | solution.py:91
  488.7 186.5 %collective-permute-start.59 = (bf16[64,2048]{1,0:T(8,128)(2,1)}, bf16[64,2048]{1,0:T(8,128)(2,1)}, u32[]{:S(2)}, u32[]{:S(2)}) collective-permute-start(bf16[64,2048]{1,0:T(8,128)(2,1)} %get-tuple-element.120), channel_id=1, source_target_pairs={{0,2},{1,3},{2,4},{3,5},{4,6},{5,7},{8,10},{9,11},{10,12},{11,13},... | collective-permute-start | bytes 786440 | tf_op jit(solution)/shard_map/ppermute | solution.py:111
  505.0 170.2 %collective-permute-start.62 = (bf16[64,2048]{1,0:T(8,128)(2,1)}, bf16[64,2048]{1,0:T(8,128)(2,1)}, u32[]{:S(2)}, u32[]{:S(2)}) collective-permute-start(bf16[64,2048]{1,0:T(8,128)(2,1)} %fusion.74), channel_id=1, source_target_pairs={{2,0},{3,1},{4,2},{5,3},{6,4},{7,5},{10,8},{11,9},{12,10},{13,11},... | collective-permute-start | bytes 786440 | tf_op jit(solution)/shard_map/ppermute | solution.py:112
  619.2 262.1 %collective-permute-start.63 = (bf16[4,256,2048]{2,1,0:T(8,128)(2,1)}, bf16[4,256,2048]{2,1,0:T(8,128)(2,1)}, u32[]{:S(2)}, u32[]{:S(2)}) collective-permute-start(bf16[4,256,2048]{2,1,0:T(8,128)(2,1)} %dynamic-slice_bitcast_fusion.1), channel_id=1, source_target_pairs={{0,1},{1,0},{2,3},{3,2},{4,5},{5,4},{6,7},{7,6},{8,9},{9,8},{10,11... | collective-permute-start | bytes 12582920 | tf_op jit(solution)/shard_map/ppermute | solution.py:101
  635.0 188.8 %collective-permute-start.46 = (bf16[4,256,1536]{2,1,0:T(8,128)(2,1)}, bf16[4,256,1536]{2,1,0:T(8,128)(2,1)}, u32[]{:S(2)}, u32[]{:S(2)}) collective-permute-start(bf16[4,256,1536]{2,1,0:T(8,128)(2,1)} %dynamic-slice_bitcast_fusion.2), channel_id=1, source_target_pairs={{0,1},{1,0},{2,3},{3,2},{4,5},{5,4},{6,7},{7,6},{8,9},{9,8},{10,11... | collective-permute-start | bytes 9437192 | tf_op jit(solution)/shard_map/ppermute | solution.py:101
  653.8 165.7 %collective-permute-start.37 = (bf16[256,2048]{0,1:T(8,128)(2,1)}, bf16[256,2048]{0,1:T(8,128)(2,1)}, u32[]{:S(2)}, u32[]{:S(2)}) collective-permute-start(bf16[256,2048]{0,1:T(8,128)(2,1)} %bitcast.477), channel_id=1, source_target_pairs={{0,8},{8,0},{16,24},{24,16},{1,9},{9,1},{17,25},{25,17},{2,10},{10... | collective-permute-start | bytes 3145736 | tf_op jit(solution)/shard_map/ppermute | solution.py:74
  675.1 146.3 %collective-permute-start.38 = (bf16[256,2048]{0,1:T(8,128)(2,1)}, bf16[256,2048]{0,1:T(8,128)(2,1)}, u32[]{:S(2)}, u32[]{:S(2)}) collective-permute-start(bf16[256,2048]{0,1:T(8,128)(2,1)} %bitcast.481), channel_id=1, source_target_pairs={{0,16},{8,24},{16,0},{24,8},{1,17},{9,25},{17,1},{25,9},{2,18},{10... | collective-permute-start | bytes 3145736 | tf_op jit(solution)/shard_map/ppermute | solution.py:74
  675.2 147.8 %collective-permute-start.39 = (bf16[256,2048]{0,1:T(8,128)(2,1)}, bf16[256,2048]{0,1:T(8,128)(2,1)}, u32[]{:S(2)}, u32[]{:S(2)}) collective-permute-start(bf16[256,2048]{0,1:T(8,128)(2,1)} %bitcast.478), channel_id=1, source_target_pairs={{0,24},{8,16},{16,8},{24,0},{1,25},{9,17},{17,9},{25,1},{2,26},{10... | collective-permute-start | bytes 3145736 | tf_op jit(solution)/shard_map/ppermute | solution.py:74
  819.5 70.6 %collective-permute-start.73 = (bf16[4,256,2048]{2,1,0:T(8,128)(2,1)}, bf16[4,256,2048]{2,1,0:T(8,128)(2,1)S(1)}, u32[]{:S(2)}, u32[]{:S(2)}) collective-permute-start(bf16[4,256,2048]{2,1,0:T(8,128)(2,1)} %dynamic-slice_bitcast_fusion), channel_id=1, source_target_pairs={{0,1},{1,0},{2,3},{3,2},{4,5},{5,4},{6,7},{7,6},{8,9},{9,8},{10,11... | collective-permute-start | bytes 12582920 | tf_op jit(solution)/shard_map/ppermute | solution.py:101
  943.3 69.7 %collective-permute-start.49 = (bf16[256,1536]{1,0:T(8,128)(2,1)S(1)}, bf16[256,1536]{1,0:T(8,128)(2,1)S(1)}, u32[]{:S(2)}, u32[]{:S(2)}) collective-permute-start(bf16[256,1536]{1,0:T(8,128)(2,1)S(1)} %get-tuple-element.102), channel_id=1, source_target_pairs={{0,2},{1,3},{2,4},{3,5},{4,6},{5,7},{8,10},{9,11},{10,12},{11,13},... | collective-permute-start | bytes 2359304 | tf_op jit(solution)/shard_map/ppermute | solution.py:111
  948.2 55.4 %collective-permute-start.75 = (bf16[256,2048]{1,0:T(8,128)(2,1)S(1)}, bf16[256,2048]{1,0:T(8,128)(2,1)S(1)}, u32[]{:S(2)}, u32[]{:S(2)}) collective-permute-start(bf16[256,2048]{1,0:T(8,128)(2,1)S(1)} %fusion.27), channel_id=1, source_target_pairs={{0,2},{1,3},{2,4},{3,5},{4,6},{5,7},{8,10},{9,11},{10,12},{11,13},... | collective-permute-start | bytes 3145736 | tf_op jit(solution)/shard_map/ppermute | solution.py:111
  952.3 60.7 %collective-permute-start.52 = (bf16[256,1536]{1,0:T(8,128)(2,1)S(1)}, bf16[256,1536]{1,0:T(8,128)(2,1)S(1)}, u32[]{:S(2)}, u32[]{:S(2)}) collective-permute-start(bf16[256,1536]{1,0:T(8,128)(2,1)S(1)} %fusion.48), channel_id=1, source_target_pairs={{2,0},{3,1},{4,2},{5,3},{6,4},{7,5},{10,8},{11,9},{12,10},{13,11},... | collective-permute-start | bytes 2359304 | tf_op jit(solution)/shard_map/ppermute | solution.py:112
  967.9 55.1 %collective-permute-start.68 = (bf16[256,2048]{1,0:T(8,128)(2,1)}, bf16[256,2048]{1,0:T(8,128)(2,1)}, u32[]{:S(2)}, u32[]{:S(2)}) collective-permute-start(bf16[256,2048]{1,0:T(8,128)(2,1)} %get-tuple-element.83), channel_id=1, source_target_pairs={{2,0},{3,1},{4,2},{5,3},{6,4},{7,5},{10,8},{11,9},{12,10},{13,11},... | collective-permute-start | bytes 3145736 | tf_op jit(solution)/shard_map/ppermute | solution.py:112
  (155 other events, 4152.0 us)
Sparse Core Ops, SparseCore 0:
  677.5 137.7 all-reduce.3

commit v2 on v1

v2 whole, which is shorter than its diff:
```python
import functools

import jax
import jax.numpy as jnp
from jax import lax
from jax.experimental import pallas as pl
from jax.experimental.pallas import tpu as pltpu
from jax.sharding import PartitionSpec as P

HEADS = 8
ROT = 64
CORES = 2
LANES = 128
BF = jnp.bfloat16
F32 = jnp.float32
MESH = pl.DeviceIdType.MESH


def nn(left, right):
    return jnp.dot(left, right, preferred_element_type=F32)


def nt(left, right):
    return lax.dot_general(left, right, (((1,), (1,)), ((), ())), preferred_element_type=F32)


def tn(left, right):
    return lax.dot_general(left, right, (((0,), (0,)), ((), ())), preferred_element_type=F32)


def turn_tables(length):
    inverse = 10000.0 ** (-jnp.arange(0, ROT, 2, dtype=F32) / ROT)
    angle = jnp.arange(length, dtype=F32)[:, None] * inverse[None, :]
    cosine, sine = jnp.cos(angle), jnp.sin(angle)
    rest = jnp.zeros((length, LANES - ROT), F32)
    return jnp.stack(
        [
            jnp.concatenate([cosine, cosine, rest + 1.0], axis=1),
            jnp.concatenate([sine, sine, rest], axis=1),
        ]
    )


def kernel(n, m, dims, names, *refs):
    ref = dict(zip(names, refs))
    rows, width, piece, part, hidden, heads, head_size = dims
    line = m // CORES
    hops = line - 1
    length = rows * n
    scale = head_size ** (-0.5)
    s, d = lax.axis_index("seq"), lax.axis_index("dp")
    z, c = d // CORES, d % CORES
    other = z * CORES + 1 - c
    drains = []

    def remote(src, dst, send, recv, device):
        return pltpu.make_async_remote_copy(
            src_ref=src, dst_ref=dst, send_sem=send, recv_sem=recv, device_id=device, device_id_type=MESH
        )

    def push(src, dst, send, recv, device, when=None):
        copy = remote(src, dst, send, recv, device)
        if when is None:
            copy.start()
        else:
            pl.when(when)(copy.start)
        drains.append((copy, when))

    def arrived(dst, recv):
        remote(dst, dst, recv, recv, {"dp": other}).wait_recv()

    def local(src, dst, sem):
        copy = pltpu.make_async_copy(src, dst, sem)
        copy.start()
        return copy

    def block(buffer, index, size, offset=0, count=None):
        count = size if count is None else count
        return buffer.at[pl.ds(pl.multiple_of(index * size + offset, count), count)]

    barrier = pltpu.get_barrier_semaphore()

    def greet(device):
        pl.semaphore_signal(barrier, inc=1, device_id=device, device_id_type=MESH)

    for k in range(1, n):
        greet({"seq": (s + k) % n})
    greet({"dp": other})
    pl.when(z > 0)(lambda: greet({"dp": d - CORES}))
    pl.when(z < line - 1)(lambda: greet({"dp": d + CORES}))
    pl.semaphore_wait(barrier, n + (z + line - 1) // line + 1 - (z + 1) // line)

    seq_send, seq_recv = ref["seq_send"], ref["seq_recv"]

    def seq_push(item, src, dst):
        for k in range(1, n):
            j = (s + k) % n
            push(src(j), dst, seq_send.at[item, k], seq_recv.at[item, k], {"seq": j})

    def seq_wait(item, dst):
        for k in range(1, n):
            arrived(dst((s - k + n) % n), seq_recv.at[item, k])

    square = n == 4
    beside, across = s + 1 - 2 * (s % 2), (s + 2) % n
    corner = n - 1 - s

    def halves(item, buffer, owner, half):
        return block(buffer, owner, rows, half * (rows // 2), rows // 2)

    def spread_first(item, buffer):
        mine = block(buffer, s, rows)
        if not square:
            seq_push(item, lambda j: mine, mine)
            return
        push(mine, mine, seq_send.at[item, 0], seq_recv.at[item, 0], {"seq": beside})
        push(mine, mine, seq_send.at[item, 1], seq_recv.at[item, 1], {"seq": across})

    def spread_second(item, buffer):
        if not square:
            return
        arrived(block(buffer, beside, rows), seq_recv.at[item, 0])
        part_one = halves(item, buffer, beside, 0)
        push(part_one, part_one, seq_send.at[item, 2], seq_recv.at[item, 2], {"seq": across})
        arrived(block(buffer, across, rows), seq_recv.at[item, 1])
        part_two = halves(item, buffer, across, 1)
        push(part_two, part_two, seq_send.at[item, 3], seq_recv.at[item, 3], {"seq": beside})

    def spread_wait(item, buffer):
        if not square:
            seq_wait(item, lambda j: block(buffer, j, rows))
            return
        arrived(halves(item, buffer, corner, 0), seq_recv.at[item, 2])
        arrived(halves(item, buffer, corner, 1), seq_recv.at[item, 3])

    dense_rows, mid_rows, shrink_rows = part // m, width // m, hidden // m
    chains = {
        "dense": (0, ref["dense_all"], dense_rows, 0, dense_rows),
        "joint_a": (1, ref["joint_all"], mid_rows, 0, mid_rows // 2),
        "joint_b": (2, ref["joint_all"], mid_rows, mid_rows // 2, mid_rows // 2),
        "expand_a": (3, ref["expand_all"], mid_rows, 0, mid_rows // 2),
        "expand_b": (4, ref["expand_all"], mid_rows, mid_rows // 2, mid_rows // 2),
        "shrink_a": (5, ref["shrink_all"], shrink_rows, 0, shrink_rows // 2),
        "shrink_b": (6, ref["shrink_all"], shrink_rows, shrink_rows // 2, shrink_rows // 2),
    }
    ag_send, ag_recv = ref["ag_send"], ref["ag_recv"]
    swap_send, swap_recv = ref["swap_send"], ref["swap_recv"]

    def shard(name, owner):
        _, buffer, size, offset, count = chains[name]
        return block(buffer, owner, size, offset, count)

    def gather_step(name, hop):
        number = chains[name][0]

        def swap(owner, when=None):
            view = shard(name, owner * CORES + c)
            push(
                view,
                view,
                swap_send.at[number, owner],
                swap_recv.at[number, owner],
                {"dp": other},
                when,
            )

        def forward(side, owner, when):
            view = shard(name, owner * CORES + c)
            push(
                view,
                view,
                ag_send.at[number, side, hop],
                ag_recv.at[number, side, hop],
                {"dp": d + CORES if side == 0 else d - CORES},
                when,
            )

        if hop == 0:
            forward(0, z, z < line - 1)
            forward(1, z, z > 0)
            swap(z)
            return
        for side, owner, valid, more in (
            (0, z - hop, z >= hop, z < line - 1),
            (1, z + hop, z + hop < line, z > 0),
        ):
            owner = (owner + line) % line
            view = shard(name, owner * CORES + c)
            pl.when(valid)(functools.partial(arrived, view, ag_recv.at[number, side, hop - 1]))
            if hop < hops:
                forward(side, owner, valid & more)
            swap(owner, valid)

    def gather_wait(name):
        for owner in range(line):
            arrived(shard(name, owner * CORES + 1 - c), swap_recv.at[chains[name][0], owner])

    groups = (("dense", "joint_a", "joint_b"), ("expand_a", "expand_b"), ("shrink_a", "shrink_b"))
    gather_queue = []
    for index, group in enumerate(groups):
        following = groups[index + 1] if index + 1 < len(groups) else ()
        for hop in range(1, hops + 1):
            for place, name in enumerate(group):
                gather_queue.append((name, hop))
                if hop == hops and place < len(following):
                    gather_queue.append((following[place], 0))

    def gather(upto):
        while gather_queue:
            entry = gather_queue.pop(0)
            gather_step(*entry)
            if entry == upto:
                return

    sums = {
        "dense": (0, "dense", 0, dense_rows, width),
        "joint_a": (1, "joint", 0, mid_rows // 2, 3 * part),
        "joint_b": (2, "joint", mid_rows // 2, mid_rows // 2, 3 * part),
        "expand_a": (3, "expand", 0, mid_rows // 2, hidden),
        "expand_b": (4, "expand", mid_rows // 2, mid_rows // 2, hidden),
        "shrink_a": (5, "shrink", 0, shrink_rows // 2, width),
        "shrink_b": (6, "shrink", shrink_rows // 2, shrink_rows // 2, width),
    }
    core_send, core_recv = ref["core_send"], ref["core_recv"]
    rs_send, rs_recv = ref["rs_send"], ref["rs_recv"]
    adds, add_sem = ref["adds"], ref["add_sem"]

    def reduce_start(name):
        number, kind, offset, count, _ = sums[name]
        push(
            ref[kind + "_sum"].at[:, 1 - c, pl.ds(offset, count)],
            ref[kind + "_core"].at[:, pl.ds(offset, count)],
            core_send.at[number],
            core_recv.at[number],
            {"dp": other},
        )

    def added(sources, count, columns, into):
        copies = []
        for slot, source in enumerate(sources):
            copies.append(local(source, adds.at[slot, pl.ds(0, count), pl.ds(0, columns)], add_sem.at[slot]))
        for copy in copies:
            copy.wait()

        @pl.loop(0, count // 16)
        def _(i):
            at = pl.ds(pl.multiple_of(i * 16, 16), 16)
            total = adds[0, at, 0:columns].astype(F32)
            for slot in range(1, len(sources)):
                total = total + adds[slot, at, 0:columns].astype(F32)
            into(at, total)

    def reduce_hop(name, hop):
        number, kind, offset, count, columns = sums[name]
        at = pl.ds(offset, count)
        held, core, chain = ref[kind + "_sum"], ref[kind + "_core"], ref[kind + "_chain"]
        if hop == 1:
            arrived(core.at[:, at], core_recv.at[number])

        def keep(where, total):
            adds[0, where, 0:columns] = total.astype(BF)

        for side, target, valid, joined in (
            (0, z + line - hop, z < hop, z > 0),
            (1, z - line + hop, z + hop >= line, z < line - 1),
        ):
            target = (target + line) % line
            mine, theirs = held.at[target, c, at], core.at[target, at]
            behind = chain.at[side, target, at]

            @pl.when(valid)
            def _():
                if hop > 1:

                    @pl.when(joined)
                    def _():
                        arrived(behind, rs_recv.at[number, side, hop - 2])
                        added((mine, theirs, behind), count, columns, keep)

                    @pl.when(jnp.logical_not(joined))
                    def _():
                        added((mine, theirs), count, columns, keep)
                else:
                    added((mine, theirs), count, columns, keep)
                local(adds.at[0, pl.ds(0, count), pl.ds(0, columns)], mine, add_sem.at[0]).wait()

            push(
                mine,
                behind,
                rs_send.at[number, side, hop - 1],
                rs_recv.at[number, side, hop - 1],
                {"dp": d + CORES if side == 0 else d - CORES},
                valid,
            )

    def reduce_last(name, into):
        number, kind, offset, count, columns = sums[name]
        at = pl.ds(offset, count)
        held, core, chain = ref[kind + "_sum"], ref[kind + "_core"], ref[kind + "_chain"]
        mine, theirs = held.at[z, c, at], core.at[z, at]
        below, above = chain.at[0, z, at], chain.at[1, z, at]

        @pl.when(z > 0)
        def _():
            arrived(below, rs_recv.at[number, 0, hops - 1])

        @pl.when(z < line - 1)
        def _():
            arrived(above, rs_recv.at[number, 1, hops - 1])

        @pl.when(z == 0)
        def _():
            added((mine, theirs, above), count, columns, into)

        @pl.when(z == line - 1)
        def _():
            added((mine, theirs, below), count, columns, into)

        @pl.when((z > 0) & (z < line - 1))
        def _():
            added((mine, theirs, below, above), count, columns, into)

    def finish_direct(name, out):
        _, _, offset, count, columns = sums[name]

        def keep(where, total):
            ref["wide_one"][where, 0:columns] = total

        reduce_last(name, keep)
        local(ref["wide_one"].at[pl.ds(0, count), pl.ds(0, columns)], out.at[pl.ds(offset, count)], add_sem.at[0]).wait()

    def finish_exchange(name, item, out):
        _, kind, offset, count, columns = sums[name]
        done = ref[kind + "_done"]

        def keep(where, total):
            adds[0, where, 0:columns] = total.astype(BF)

        reduce_last(name, keep)
        local(adds.at[0, pl.ds(0, count), pl.ds(0, columns)], done.at[pl.ds(offset, count)], add_sem.at[0]).wait()
        for j in range(offset // piece, (offset + count) // piece):
            view = done.at[pl.ds(j * piece, piece)]
            k = (j - s + n) % n
            mine = block(out, s, piece)
            push(view, mine, seq_send.at[item, k], seq_recv.at[item, k], {"seq": j}, k != 0)

            @pl.when(k == 0)
            def _():
                local(view, mine, add_sem.at[0]).wait()

    upstream, normed = ref["upstream"], ref["normed"]
    qkv, gate, mixed, grad_qkv = ref["qkv"], ref["gate"], ref["mixed"], ref["grad_qkv"]
    act, slope = ref["act"], ref["slope"]
    left, right, dense = ref["left"], ref["right"], ref["dense"]
    wide_one, wide_two = ref["wide_one"], ref["wide_two"]
    stage, stage_sem, load_sem = ref["stage"], ref["stage_sem"], ref["load_sem"]
    x_sem = ref["x_sem"]
    gains, tables = ref["gains"], ref["tables"]
    small = 32

    def tile(i, size=rows):
        return pl.ds(pl.multiple_of(i * size, size), size)

    def each_tile(body):
        load = lambda i: local(ref["tokens_all"].at[pl.ds(i * rows, rows)], stage.at[i % 2, pl.ds(0, rows), pl.ds(0, width)], x_sem.at[i % 2])
        copy = load(0)
        for i in range(n):
            copy.wait()
            if i + 1 < n:
                copy = load(i + 1)
            body(i, i % 2)

    def normal_of(slot, at):
        value = stage[slot, at, 0:width].astype(F32)
        center = value - jnp.mean(value, axis=-1, keepdims=True)
        return center * lax.rsqrt(jnp.mean(center * center, axis=-1, keepdims=True) + 1e-05)

    def norm_stage(which):
        def body(i, slot):
            @pl.loop(0, rows // small)
            def _(j):
                value = normal_of(slot, tile(j, small))
                value = value * gains[2 * which : 2 * which + 1, :] + gains[2 * which + 1 : 2 * which + 2, :]
                at = pl.ds(pl.multiple_of(i * rows + j * small, small), small)
                normed[at, :] = value.astype(BF)

        each_tile(body)

    def turn(value, at, sign):
        head = value[:, :LANES]
        lane = lax.broadcasted_iota(jnp.int32, head.shape, 1)
        lower = -sign * pltpu.roll(head, LANES - ROT // 2, 1)
        upper = sign * pltpu.roll(head, ROT // 2, 1)
        head = head * tables[0, at, :] + jnp.where(lane < ROT // 2, lower, upper) * tables[1, at, :]
        if value.shape[1] == LANES:
            return head
        return jnp.concatenate([head, value[:, LANES:]], axis=1)

    def joint_stage():
        @pl.loop(0, n)
        def _(i):
            at = tile(i)
            joint = nn(normed[at, :], right[0:width, 0 : 3 * part]) + ref["joint_bias"][...]
            for kind in range(3):
                for head in range(heads):
                    first = kind * part + head * head_size
                    value = joint[:, first : first + head_size]
                    if kind < 2:
                        value = turn(value, at, 1.0)
                    qkv[at, first : first + head_size] = value.astype(BF)

    def gate_stage():
        @pl.loop(0, n)
        def _(i):
            gate[tile(i), :] = nt(upstream[tile(i), :], dense[...]).astype(BF)

    query_tile = rows
    grad_key, grad_value = wide_one, wide_two

    def attend_tile(head, i):
        keys = (i + 1) * query_tile
        at = pl.ds(i * query_tile, query_tile)
        seen = pl.ds(0, keys)
        q_at = pl.ds(head * head_size, head_size)
        k_at = pl.ds(part + head * head_size, head_size)
        v_at = pl.ds(2 * part + head * head_size, head_size)
        query = qkv[at, q_at]
        scores = nt(query, qkv[seen, k_at]) * scale
        row = lax.broadcasted_iota(jnp.int32, (query_tile, keys), 0) + i * query_tile
        column = lax.broadcasted_iota(jnp.int32, (query_tile, keys), 1)
        scores = jnp.where(column <= row, scores, -1e30)
        expo = jnp.exp(scores - jnp.max(scores, axis=-1, keepdims=True))
        probs = expo / jnp.sum(expo, axis=-1, keepdims=True)
        low = probs.astype(BF)
        mixed[at, q_at] = nn(low, qkv[seen, v_at]).astype(BF)
        back = gate[at, q_at]
        grad_probs = nt(back, qkv[seen, v_at])
        inner = jnp.sum(probs * grad_probs, axis=-1, keepdims=True)
        grad_scores = (probs * (grad_probs - inner)).astype(BF)
        grad_query = nn(grad_scores, qkv[seen, k_at]) * scale
        grad_qkv[at, q_at] = turn(grad_query, at, -1.0).astype(BF)
        key_part, value_part = tn(grad_scores, query), tn(low, back)
        for b in range(i + 1):
            here = (slice(0, rows), slice(b * head_size, (b + 1) * head_size))
            for total, added_part in ((grad_key, key_part), (grad_value, value_part)):
                added_part = added_part[b * rows : (b + 1) * rows]
                total[here] = added_part if i == n - 1 else total[here] + added_part

    def attend_stage(head):
        for i in range(n - 1, -1, -1):
            attend_tile(head, i)

        for b in range(n):
            at = pl.ds(b * rows, rows)
            here = (slice(0, rows), slice(b * head_size, (b + 1) * head_size))
            k_at = pl.ds(part + head * head_size, head_size)
            v_at = pl.ds(2 * part + head * head_size, head_size)
            grad_qkv[at, k_at] = turn(grad_key[here] * scale, at, -1.0).astype(BF)
            grad_qkv[at, v_at] = grad_value[here].astype(BF)

    def weight_grad(kind, left_of, right_of, count, columns):
        out = ref[kind + "_sum"]

        def stored(b, slot):
            return pltpu.make_async_copy(
                stage.at[slot, pl.ds(0, count), pl.ds(0, columns)],
                out.at[b // CORES, b % CORES],
                stage_sem.at[slot],
            )

        @pl.loop(0, m)
        def _(b):
            slot = b % 2

            @pl.when(b >= 2)
            def _():
                stored(b - 2, slot).wait()

            stage[slot, 0:count, 0:columns] = tn(left_of(b), right_of()).astype(BF)
            stored(b, slot).start()

        for b in range(max(m - 2, 0), m):
            stored(b, b % 2).wait()

    def dense_grad_stage():
        out = ref["dense_sum"]
        wide = min(part, stage.shape[1])
        for first in range(0, part, wide):
            stage[0, 0:wide, 0:width] = tn(mixed[:, first : first + wide], upstream[...]).astype(BF)
            copies = []
            for b in range(wide // dense_rows):
                owner = first // dense_rows + b
                copies.append(
                    local(
                        stage.at[0, pl.ds(b * dense_rows, dense_rows), pl.ds(0, width)],
                        out.at[owner // CORES, owner % CORES],
                        ref["dense_sem"].at[b],
                    )
                )
            for copy in copies:
                copy.wait()

    def columns_of(buffer, count):
        return lambda b: buffer[:, pl.ds(pl.multiple_of(b * count, LANES), count)]

    def expand_stage(start, stop):
        @pl.loop(start, stop)
        def _(i):
            wide_one[:, 0:hidden] = nn(normed[tile(i), :], left[...]) + ref["expand_bias"][...]

            @pl.loop(0, rows // small)
            def _(j):
                value = wide_one[tile(j, small), 0:hidden]
                share = 0.5 * (1.0 + lax.erf(value * 0.7071067811865476))
                density = jnp.exp(-0.5 * value * value) * 0.3989422804014327
                at = pl.ds(pl.multiple_of(i * rows + j * small, small), small)
                act[at, :] = (value * share).astype(BF)
                slope[at, :] = (share + value * density).astype(BF)

    def shrink_stage(start, stop):
        @pl.loop(start, stop)
        def _(i):
            wide_one[:, 0:hidden] = nt(upstream[tile(i), :], right[0:hidden, 0:width])

            @pl.loop(0, rows // small)
            def _(j):
                at = pl.ds(pl.multiple_of(i * rows + j * small, small), small)
                grad = (wide_one[tile(j, small), 0:hidden] * slope[at, :].astype(F32)).astype(BF)
                slope[at, :] = grad
                ref["expand_total"][...] += jnp.sum(grad.astype(F32), axis=0, keepdims=True)

    def owner_push(item, source, out, i):
        k = (i - s + n) % n
        mine = block(out, s, rows)
        push(source, mine, seq_send.at[item, k], seq_recv.at[item, k], {"seq": i}, k != 0)

        @pl.when(k == 0)
        def _():
            local(source, mine, add_sem.at[0]).wait()

    def output_stage(i):
        at = pl.ds(i * rows, rows)
        total = nn(mixed[at, :], dense[...]) + nn(act[at, :], right[0:hidden, 0:width])
        stage[i % 2, 0:rows, 0:width] = total.astype(BF)
        local(stage.at[i % 2, pl.ds(0, rows), pl.ds(0, width)], ref["output_part"].at[at], stage_sem.at[0]).wait()
        owner_push(4, ref["output_part"].at[at], ref["output_all"], i)

    def input_stage(i, slot):
        at = pl.ds(i * rows, rows)
        wide_one[:, 0:width] = nt(grad_qkv[at, :], right[0:width, 0 : 3 * part])
        wide_two[...] = nt(slope[at, :], left[...])

        @pl.loop(0, rows // small)
        def _(j):
            here = tile(j, small)
            normal = normal_of(slot, here)
            grad_one, grad_two = wide_one[here, 0:width], wide_two[here, :]
            total = grad_one * gains[0:1, :] + grad_two * gains[2:3, :]
            normed[pl.ds(pl.multiple_of(i * rows + j * small, small), small), :] = total.astype(BF)
            gain_total = ref["gain_total"]
            gain_total[0:1, :] += jnp.sum(grad_one * normal, axis=0, keepdims=True)
            gain_total[1:2, :] += jnp.sum(grad_one, axis=0, keepdims=True)
            gain_total[2:3, :] += jnp.sum(grad_two * normal, axis=0, keepdims=True)
            gain_total[3:4, :] += jnp.sum(grad_two, axis=0, keepdims=True)

        owner_push(5, normed.at[at], ref["input_all"], i)

    ref["gain_total"][...] = jnp.zeros_like(ref["gain_total"])
    ref["joint_total"][...] = jnp.zeros_like(ref["joint_total"])
    ref["expand_total"][...] = jnp.zeros_like(ref["expand_total"])
    own = [
        local(ref["dense_own"], block(ref["dense_all"], d, dense_rows), load_sem.at[0]),
        local(ref["joint_own"].at[s], joint_block := block(ref["joint_all"], d * n + s, piece), load_sem.at[1]),
        local(ref["expand_own"].at[s], expand_block := block(ref["expand_all"], d * n + s, piece), load_sem.at[2]),
        local(ref["shrink_own"], block(ref["shrink_all"], d, shrink_rows), load_sem.at[3]),
        local(ref["tokens"], block(ref["tokens_all"], s, rows), load_sem.at[4]),
        local(ref["cotangent"], block(upstream, s, rows), load_sem.at[5]),
    ]
    seq_push(0, lambda j: ref["joint_own"].at[j], joint_block)
    for copy in own:
        copy.wait()
    gather_step("dense", 0)
    seq_wait(0, lambda j: block(ref["joint_all"], d * n + j, piece))
    gather_step("joint_a", 0)
    gather_step("joint_b", 0)
    spread_first(2, ref["tokens_all"])
    seq_push(1, lambda j: ref["expand_own"].at[j], expand_block)
    gather(("dense", 1))
    spread_second(2, ref["tokens_all"])
    spread_first(3, upstream)
    gather(("joint_b", 1))
    seq_wait(1, lambda j: block(ref["expand_all"], d * n + j, piece))
    spread_wait(2, ref["tokens_all"])
    gather(("joint_b", 2) if hops > 2 else ("joint_b", hops))
    norm_stage(0)
    spread_second(3, upstream)
    gather(("joint_b", hops))
    for name in groups[0]:
        gather_wait(name)
    load_joint = local(ref["joint_all"], right.at[pl.ds(0, width), pl.ds(0, 3 * part)], load_sem.at[0])
    load_dense = local(ref["dense_all"], dense, load_sem.at[1])
    load_joint.wait()
    joint_stage()
    spread_wait(3, upstream)
    load_dense.wait()
    gather(("expand_b", 1))
    gate_stage()
    for head in range(heads):
        attend_stage(head)
        if head == 0:
            gather(("expand_b", 2) if hops > 2 else ("expand_b", hops))
    dense_grad_stage()
    reduce_start("dense")
    gather(("shrink_b", 0))
    weight_grad("joint", columns_of(normed, mid_rows), lambda: grad_qkv[...], mid_rows, 3 * part)
    reduce_start("joint_a")
    reduce_start("joint_b")

    @pl.loop(0, n)
    def _(i):
        ref["joint_total"][...] += jnp.sum(grad_qkv[tile(i), :].astype(F32), axis=0, keepdims=True)

    for name in ("expand_a", "expand_b"):
        gather_wait(name)
    load_expand = local(ref["expand_all"], left, load_sem.at[0])
    norm_stage(1)
    load_expand.wait()
    for name in ("dense", "joint_a", "joint_b"):
        reduce_hop(name, 1)
    expand_stage(0, n // 2)
    gather(("shrink_b", 1))
    expand_stage(n // 2, n)
    for name in ("dense", "joint_a", "joint_b"):
        reduce_hop(name, 2)
    weight_grad("shrink", columns_of(act, shrink_rows), lambda: upstream[...], shrink_rows, width)
    reduce_start("shrink_a")
    reduce_start("shrink_b")
    for hop in range(3, hops + 1):
        for name in ("dense", "joint_a", "joint_b"):
            reduce_hop(name, hop)
    gather(("shrink_b", 2) if hops > 2 else ("shrink_b", hops))
    reduce_hop("shrink_a", 1)
    reduce_hop("shrink_b", 1)
    gather(("shrink_b", hops))
    for name in ("shrink_a", "shrink_b"):
        gather_wait(name)
    local(ref["shrink_all"], right.at[pl.ds(0, hidden), pl.ds(0, width)], load_sem.at[0]).wait()
    shrink_stage(0, n)
    reduce_hop("shrink_a", 2)
    reduce_hop("shrink_b", 2)
    weight_grad("expand", columns_of(normed, mid_rows), lambda: slope[...], mid_rows, hidden)
    reduce_start("expand_a")
    reduce_start("expand_b")
    for hop in range(3, hops + 1):
        for name in ("shrink_a", "shrink_b"):
            reduce_hop(name, hop)
    finish_direct("dense", ref["dense_grad"])
    finish_exchange("joint_a", 6, ref["joint_grad"])
    finish_exchange("joint_b", 6, ref["joint_grad"])
    for i in range(n // 2):
        output_stage(i)
    reduce_hop("expand_a", 1)
    reduce_hop("expand_b", 1)
    for i in range(n // 2, n):
        output_stage(i)
    load_joint = local(ref["joint_all"], right.at[pl.ds(0, width), pl.ds(0, 3 * part)], load_sem.at[0])
    reduce_hop("expand_a", 2)
    reduce_hop("expand_b", 2)
    load_joint.wait()
    each_tile(input_stage)
    for hop in range(3, hops + 1):
        for name in ("expand_a", "expand_b"):
            reduce_hop(name, hop)
    finish_direct("shrink_a", ref["shrink_grad"])
    finish_direct("shrink_b", ref["shrink_grad"])
    finish_exchange("expand_a", 7, ref["expand_grad"])
    finish_exchange("expand_b", 7, ref["expand_grad"])
    seq_wait(4, lambda j: block(ref["output_all"], j, rows))
    seq_wait(5, lambda j: block(ref["input_all"], j, rows))
    seq_wait(6, lambda j: block(ref["joint_grad"], j, piece))
    seq_wait(7, lambda j: block(ref["expand_grad"], j, piece))
    for copy, when in drains:
        if when is None:
            copy.wait_send()
        else:
            pl.when(when)(copy.wait_send)


def run_kernel(n, m, dims, inputs):
    rows, width, piece, part, hidden, heads, head_size = dims
    line, length = m // CORES, rows * n
    hops = line - 1
    dense_rows, mid_rows, shrink_rows = part // m, width // m, hidden // m
    high = max(rows, mid_rows, shrink_rows)
    broad = max(width, hidden, 3 * part)
    anywhere, vmem = pl.BlockSpec(memory_space=pl.ANY), pl.BlockSpec(memory_space=pltpu.VMEM)
    outputs = {
        "output_all": ((length, width), BF),
        "input_all": ((length, width), BF),
        "dense_grad": ((dense_rows, width), F32),
        "shrink_grad": ((shrink_rows, width), F32),
        "joint_grad": ((n * piece, 3 * part), BF),
        "expand_grad": ((n * piece, hidden), BF),
        "gain_total": ((4, width), F32),
        "joint_total": ((1, 3 * part), F32),
        "expand_total": ((1, hidden), F32),
        "dense_all": ((part, width), BF),
        "joint_all": ((width, 3 * part), BF),
        "expand_all": ((width, hidden), BF),
        "shrink_all": ((hidden, width), BF),
        "tokens_all": ((length, width), BF),
        "output_part": ((length, width), BF),
        "joint_done": ((mid_rows, 3 * part), BF),
        "expand_done": ((mid_rows, hidden), BF),
    }
    shapes = {
        "dense": (dense_rows, width),
        "joint": (mid_rows, 3 * part),
        "expand": (mid_rows, hidden),
        "shrink": (shrink_rows, width),
    }
    for kind, shape in shapes.items():
        outputs[kind + "_sum"] = ((line, CORES) + shape, BF)
        outputs[kind + "_core"] = ((line,) + shape, BF)
        outputs[kind + "_chain"] = ((2, line) + shape, BF)
    in_vmem = ("gain_total", "joint_total", "expand_total")
    dma = pltpu.SemaphoreType.DMA
    scratch = {
        "upstream": pltpu.VMEM((length, width), BF),
        "normed": pltpu.VMEM((length, width), BF),
        "qkv": pltpu.VMEM((length, 3 * part), BF),
        "gate": pltpu.VMEM((length, part), BF),
        "mixed": pltpu.VMEM((length, part), BF),
        "grad_qkv": pltpu.VMEM((length, 3 * part), BF),
        "act": pltpu.VMEM((length, hidden), BF),
        "slope": pltpu.VMEM((length, hidden), BF),
        "left": pltpu.VMEM((width, hidden), BF),
        "right": pltpu.VMEM((max(width, hidden), max(width, 3 * part)), BF),
        "dense": pltpu.VMEM((part, width), BF),
        "wide_one": pltpu.VMEM((max(rows, shrink_rows // 2), max(width, hidden)), F32),
        "wide_two": pltpu.VMEM((rows, width), F32),
        "stage": pltpu.VMEM((2, high, broad), BF),
        "adds": pltpu.VMEM((4, max(mid_rows, shrink_rows) // 2, broad), BF),
        "seq_send": dma((8, max(n, 4))),
        "seq_recv": dma((8, max(n, 4))),
        "ag_send": dma((7, 2, hops)),
        "ag_recv": dma((7, 2, hops)),
        "swap_send": dma((7, line)),
        "swap_recv": dma((7, line)),
        "core_send": dma((7,)),
        "core_recv": dma((7,)),
        "rs_send": dma((7, 2, hops)),
        "rs_recv": dma((7, 2, hops)),
        "add_sem": dma((4,)),
        "stage_sem": dma((2,)),
        "load_sem": dma((6,)),
        "x_sem": dma((2,)),
        "dense_sem": dma((max(m, 8),)),
    }
    resident = ("gains", "joint_bias", "expand_bias", "tables")
    names = list(inputs) + list(outputs) + list(scratch)
    results = pl.pallas_call(
        functools.partial(kernel, n, m, dims, names),
        out_shape=[jax.ShapeDtypeStruct(shape, kind) for shape, kind in outputs.values()],
        in_specs=[vmem if name in resident else anywhere for name in inputs],
        out_specs=[vmem if name in in_vmem else anywhere for name in outputs],
        scratch_shapes=list(scratch.values()),
        compiler_params=pltpu.CompilerParams(
            collective_id=0, has_side_effects=True, vmem_limit_bytes=63 * 2**20
        ),
        cost_estimate=pl.CostEstimate(flops=10**11, bytes_accessed=10**9, transcendentals=0),
        name="block",
    )(*inputs.values())
    return dict(zip(outputs, results))


def block_plan(n, m, tokens, cotangent, shards):
    (
        first_gain,
        first_shift,
        second_gain,
        second_shift,
        joint_weight,
        joint_bias,
        dense_weight,
        dense_bias,
        expand_weight,
        expand_bias,
        shrink_weight,
        shrink_bias,
    ) = shards
    devices = n * m
    own, upstream = tokens[0], cotangent[0]
    rows, width = own.shape
    piece = width // devices
    head_size = width // HEADS
    heads = HEADS // n
    part = width // n
    hidden = expand_weight.shape[1] // n
    s = lax.axis_index("seq")

    def shuffle(values):
        shape = values.shape[:-1]
        values = values.reshape(shape + (n, m, piece))
        return jnp.swapaxes(values, -3, -2).reshape(shape + (width,))

    def unshuffle(values):
        shape = values.shape[:-1]
        values = values.reshape(shape + (m, n, piece))
        return jnp.swapaxes(values, -3, -2).reshape(shape + (width,))

    def pick(stack):
        return lax.dynamic_index_in_dim(stack, s, 0, keepdims=False)

    vectors = (
        first_gain,
        first_shift,
        second_gain,
        second_shift,
        joint_bias,
        dense_bias,
        expand_bias,
        shrink_bias,
    )
    packed = lax.all_gather(jnp.concatenate(vectors)[None], ("seq", "dp"), axis=0, tiled=True)
    full, start = [], 0
    for vector in vectors:
        full.append(packed[:, start : start + vector.shape[0]].reshape(-1).astype(F32))
        start += vector.shape[0]
    gains = shuffle(jnp.stack(full[:4]))
    joint_offset, dense_offset, expand_offset, shrink_offset = full[4:]
    inputs = {
        "tokens": shuffle(own),
        "cotangent": upstream,
        "joint_own": jnp.transpose(joint_weight.reshape(piece, 3, n, part), (2, 0, 1, 3)).reshape(
            n, piece, 3 * part
        ),
        "expand_own": jnp.swapaxes(expand_weight.reshape(piece, n, hidden), 0, 1),
        "dense_own": dense_weight,
        "shrink_own": shrink_weight,
        "gains": gains,
        "joint_bias": pick(jnp.swapaxes(joint_offset.reshape(3, n, part), 0, 1)).reshape(1, 3 * part),
        "expand_bias": pick(expand_offset.reshape(n, 1, hidden)),
        "tables": turn_tables(rows * n),
    }
    dims = (rows, width, piece, part, hidden, heads, head_size)
    got = run_kernel(n, m, dims, inputs)

    summed = jnp.sum(got["output_all"].reshape(n, rows, width).astype(F32), axis=0)
    own_wide = own.astype(F32)
    output = (own_wide + (summed + (dense_offset + shrink_offset))).astype(BF)[None]

    grad_normal = jnp.sum(got["input_all"].reshape(n, rows, width).astype(F32), axis=0)
    grad_normal = unshuffle(grad_normal)
    center = own_wide - jnp.mean(own_wide, axis=-1, keepdims=True)
    spread = lax.rsqrt(jnp.mean(center * center, axis=-1, keepdims=True) + 1e-05)
    normal = center * spread
    through = grad_normal - jnp.mean(grad_normal, axis=-1, keepdims=True)
    through = through - normal * jnp.mean(grad_normal * normal, axis=-1, keepdims=True)
    upstream_wide = upstream.astype(F32)
    grad_tokens = (upstream_wide + spread * through)[None]

    def placed(vector, groups):
        blocks = vector.reshape(groups, 1, -1)
        mine = (jnp.arange(n) == s).reshape(1, n, 1)
        return jnp.where(mine, blocks, 0.0).reshape(-1)

    gain_total = unshuffle(got["gain_total"])
    sums = (
        gain_total[0],
        gain_total[1],
        gain_total[2],
        gain_total[3],
        placed(got["joint_total"], 3),
        placed(got["expand_total"], 1),
        jnp.sum(upstream_wide, axis=0),
    )
    sums = jnp.concatenate([v.reshape(devices, -1) for v in sums], axis=1)
    sums = lax.psum_scatter(sums, ("seq", "dp"), scatter_dimension=0, tiled=True)[0]
    small, start = [], 0
    for length_of in (piece, piece, piece, piece, joint_bias.shape[0], expand_bias.shape[0], piece):
        small.append(sums[start : start + length_of])
        start += length_of

    joint_grad = got["joint_grad"].reshape(n, piece, 3, part)
    joint_grad = jnp.transpose(joint_grad, (1, 2, 0, 3)).reshape(piece, 3 * width).astype(F32)
    expand_grad = got["expand_grad"].reshape(n, piece, hidden)
    expand_grad = jnp.swapaxes(expand_grad, 0, 1).reshape(piece, n * hidden).astype(F32)
    return (
        output,
        grad_tokens,
        small[0],
        small[1],
        small[2],
        small[3],
        joint_grad,
        small[4],
        got["dense_grad"],
        small[6],
        expand_grad,
        small[5],
        got["shrink_grad"],
        small[6],
    )


def solution(mesh):
    n, m = mesh.shape["seq"], mesh.shape["dp"]

    def body(tokens, cotangent, *shards):
        return block_plan(n, m, tokens, cotangent, shards)

    both = ("seq", "dp")
    tokens = P("dp", "seq", None)
    vector, matrix = P(both), P(both, None)
    return jax.shard_map(
        body,
        mesh=mesh,
        in_specs=(tokens, tokens) + (vector,) * 4 + (matrix, vector) * 4,
        out_specs=(tokens, tokens) + (vector,) * 4 + (matrix, vector) * 4,
        check_vma=False,
    )
```

time: 1100 us -> 765 us (0.70)
  Pallas kernels: 0 us -> 538 us
  waiting for transfers between devices: 409 us -> 95.2 us
  matrix products: 169 us -> 0 us
  starting transfers between devices: 167 us -> 0.04 us
  local copies, waits for them, and re-layouts: 173 us -> 41.4 us
  other arithmetic: 112 us -> 26.4 us
    pallas_call x0 -> x1, Pallas kernels: none -> 538 us  [run_kernel(): pl.pallas_call(functools.partial(kernel, n, m, dims, names), out_shape=[j...]
    ppermute x80 -> x0, waiting for transfers between devices: 284 us -> none  [the longest x12 88.2 us: gather_dp(): downs.append(lax.ppermute(downs[-1], 'dp', self.down))]
    ppermute x80 -> x0, starting transfers between devices: 167 us -> none  [the longest x12 56.5 us: scatter_dp(): rising = lax.ppermute(first, 'dp', self.up)]
    dot_general x17 -> x0, matrix products: 160 us -> none  [the longest x4 64.4 us: mm_last(): lax.dot_general(left, right, (((1,), (1,)), ((), ())), preferred_element_...]
    convert_element_type x23 -> x0, other arithmetic: 53.8 us -> none  [the longest x4 13.7 us: scatter_dp(): held = (self.pick(parts, self.c).astype(F32) + sent.astype(F32)).astype(BF)]
    unnamed x233 -> x30, local copies, waits for them, and re-layouts: 46.7 us -> 5.62 us
    another operation x19 -> x2, other arithmetic: 33.4 us -> 1.38 us  [turn_tables(): jnp.stack([jnp.concatenate([cosine, cosine, rest + 1.0], axis=1), jnp.con...]
    unnamed x2, waiting for transfers between devices: 125 us -> 95.2 us
  transfers between devices with their start and end apart: 81 -> 1, of which waited for: 29 -> 1; matrix products, arithmetic and copies ran while one was open for 40% -> 5% of each run, Pallas kernels for 0% -> 0%
where the time goes in v2:
time: 765 us; the launch traced here: 758 us
  Pallas kernels  538 us (70%)
  waiting for transfers between devices  95.2 us (12%)
  blocking collectives  42.5 us (6%)
  local copies, waits for them, and re-layouts  41.4 us (5%)
  other arithmetic  26.4 us (3%)
  between operations  14.8 us (2%)
    pallas_call x1, Pallas kernels, run_kernel(): pl.pallas_call(functools.partial(kernel, n, m, dims, names), out_shape=[j...  538 us
    unnamed x2, waiting for transfers between devices  95.2 us
    unnamed x1, blocking collectives  42.5 us
  transfers between devices with their start and end apart: 1, of which 1 were waited for; matrix products, arithmetic and copies ran while one was open for 5% of the time, Pallas kernels for 0%

profile of v2, /device:TPU:0, one launch (start us, length us, event | category | flops | bytes accessed | tf_op | source)
XLA Modules:
  0.0 758.0 jit_solution(11913153344459389765)
XLA Ops:
  7.3 5.5 concatenate.14
  13.0 42.5 %all-reduce = bf16[26624]{0:T(1024)(128)(2,1)S(1)} all-reduce(bf16[26624]{0:T(1024)(128)(2,1)S(1)} %dynamic-update-slice), channel_id=2, replica_groups=mesh['seq'=4,'dp'=8] {'seq','dp'}, use_global_device_ids=true, to_apply=%add | all-reduce | flops 26624 | bytes 106496
  56.0 1.4 convert_reduce_fusion.3
  60.6 1.8 reshape.348.refs_2_
  62.4 1.9 fusion.11
  65.0 1.4 copy.89.refs_0_
  66.5 2.3 copy.108
  70.1 537.7 %block.1 = (bf16[1024,2048]{1,0:T(8,128)(2,1)}, bf16[1024,2048]{1,0:T(8,128)(2,1)}, f32[64,2048]{1,0:T(8,128)}, f32[256,2048]{1,0:T(8,128)}, bf16[256,1536]{1,0:...) custom-call(bf16[256,2048]{1,0:T(8,128)(2,1)} %copy.89.refs_0_, ...), custom_call_target="tpu_custom_call" | custom-call | flops 99999997952 | bytes 1000000000 | tf_op jit(solution)/shard_map/block/pallas_call | solution.py:762
  612.3 1.4 convert_reduce_fusion.1
  614.4 4.7 convert_reduce_fusion
  619.7 4.5 reduce_sum.76
  624.2 1.9 copy.90
  626.1 1.5 copy.91
  627.6 2.9 copy.92
  630.5 1.8 fusion.9
  632.7 4.4 fusion.8
  637.0 1.6 convert_bitcast_fusion.1
  638.6 1.4 reshape.366
  640.0 2.2 copy.97
  642.1 3.4 reshape.363
  645.5 1.5 copy.100
  647.0 95.2 %all-reduce.4.cloned.1.call-done = f32[32,768]{1,0:T(8,128)} async-done(((f32[32,768]{1,0:T(8,128)}), f32[32,768]{1,0:T(8,128)}) %all-reduce.4.cloned.1.call-update) | async-done | bytes 98320
  742.2 1.4 dynamic-slice_bitcast_fusion.1
  747.6 3.1 copy.121
  (83 shorter events, 15.9 us)
Async XLA Ops:
  7.2 52.4 %copy-start.8 = (bf16[64,6144]{1,0:T(8,128)(2,1)S(1)}, bf16[64,6144]{1,0:T(8,128)(2,1)}, u32[]{:S(2)}) copy-start(bf16[64,6144]{1,0:T(8,128)(2,1)} %param.20) | copy-start | bytes 2359300
  7.2 735.0 %all-reduce.4.cloned.1.call-start = ((), (), s32[]{:S(2)}) async-start(), calls=%async_computation | async-start | bytes 196608
  60.2 4.2 copy-start.1
  64.9 1.5 copy-start.3
  607.9 6.0 copy-start.2
  614.4 4.7 copy-start
  630.5 1.9 copy-start.4
  630.5 2.2 copy-start.6
  632.7 4.4 copy-start.7
  637.0 1.6 copy-start.9
  642.1 3.4 copy-start.5
  645.5 101.3 %copy-start.10 = (f32[64,2048]{1,0:T(8,128)S(1)}, f32[64,2048]{1,0:T(8,128)}, u32[]{:S(2)}) copy-start(f32[64,2048]{1,0:T(8,128)} %get-tuple-element.129) | copy-start | bytes 1572868
  743.6 7.1 copy-start.11
Sparse Core Ops, SparseCore 0:
  612.5 129.6 all-reduce.3

commit v3 on v1

v3 whole, which is shorter than its diff:
```python
import functools
import types

import jax
import jax.numpy as jnp
from jax import lax
from jax.experimental import pallas as pl
from jax.experimental.pallas import tpu as pltpu
from jax.sharding import PartitionSpec as P

HEADS = 8
ROT = 64
CORES = 2
LANES = 128
VECTOR_ROWS = 16
SEQ, DP = "seq", "dp"
BF = jnp.bfloat16
F32 = jnp.float32
MESH = pl.DeviceIdType.MESH


def nn(left, right):
    return jnp.dot(left, right, preferred_element_type=F32)


def nt(left, right):
    return lax.dot_general(left, right, (((1,), (1,)), ((), ())), preferred_element_type=F32)


def tn(left, right):
    return lax.dot_general(left, right, (((0,), (0,)), ((), ())), preferred_element_type=F32)


def turn_tables(length):
    inverse = 10000.0 ** (-jnp.arange(0, ROT, 2, dtype=F32) / ROT)
    angle = jnp.arange(length, dtype=F32)[:, None] * inverse[None, :]
    cosine, sine = jnp.cos(angle), jnp.sin(angle)
    rest = jnp.zeros((length, LANES - ROT), F32)
    return jnp.stack(
        [
            jnp.concatenate([cosine, cosine, rest + 1.0], axis=1),
            jnp.concatenate([sine, sine, rest], axis=1),
        ]
    )


def sizes_of(n, m, rows, width, feed):
    devices = n * m
    z = types.SimpleNamespace(n=n, m=m, rows=rows, width=width)
    z.line, z.hops = m // CORES, m // CORES - 1
    z.length = rows * n
    z.piece = width // devices
    z.part = width // n
    z.hidden = feed // n
    z.heads, z.head_size = HEADS // n, width // HEADS
    z.dense_rows, z.mid_rows, z.shrink_rows = z.part // m, width // m, z.hidden // m
    z.feed_pieces = feed // width
    z.high = max(rows, z.mid_rows, z.shrink_rows)
    z.broad = max(width, z.hidden, 3 * z.part)
    z.chunk = max(z.mid_rows, z.shrink_rows) // 2
    z.gain_rows = width // LANES
    z.joint_small = 5 * z.gain_rows
    z.expand_small = z.joint_small + 3 * z.part // LANES
    z.small = -(-(z.expand_small + z.hidden // LANES) // 8) * 8
    return z


def kernel(size, names, *refs):
    ref = types.SimpleNamespace(**dict(zip(names, refs)))
    n, m, line, hops = size.n, size.m, size.line, size.hops
    rows, width, piece, part, hidden = size.rows, size.width, size.piece, size.part, size.hidden
    heads, head_size, length = size.heads, size.head_size, size.length
    dense_rows, mid_rows, shrink_rows = size.dense_rows, size.mid_rows, size.shrink_rows
    scale = head_size ** (-0.5)
    s, d = lax.axis_index(SEQ), lax.axis_index(DP)
    z, c = d // CORES, d % CORES
    twin = {DP: z * CORES + 1 - c}
    above, below = {DP: d + CORES}, {DP: d - CORES}
    drains = []

    def remote(src, dst, send, recv, device):
        return pltpu.make_async_remote_copy(
            src_ref=src, dst_ref=dst, send_sem=send, recv_sem=recv, device_id=device, device_id_type=MESH
        )

    def push_all(make, when=None, keep=True):
        def start():
            pairs, _, send, recv, device = make()
            for src, dst in pairs:
                remote(src, dst, send, recv, device).start()

        def settle():
            _, whole, send, recv, device = make()
            remote(whole, whole, send, recv, device).wait_send()

        def guarded(step):
            return step if when is None else lambda: pl.when(when())(step)

        guarded(start)()
        if keep:
            drains.append(guarded(settle))
        return guarded(settle)

    def arrived(whole, recv):
        remote(whole, whole, recv, recv, twin).wait_recv()

    def local(src, dst, sem):
        copy = pltpu.make_async_copy(src, dst, sem)
        copy.start()
        return copy

    def span(index, size, count=None, offset=0):
        count = size if count is None else count
        return pl.ds(pl.multiple_of(index * size + offset, count), count)

    def lanes(index, size, offset=0):
        return pl.ds(pl.multiple_of(index * size + offset, LANES), size)

    barrier = pltpu.get_barrier_semaphore()
    greeted = [{SEQ: (s + k) % n} for k in range(1, n)]
    greeted += [{DP: (z + k) % line * CORES + c} for k in range(1, line)] + [twin]
    for device in greeted:
        pl.semaphore_signal(barrier, inc=1, device_id=device, device_id_type=MESH)
    pl.semaphore_wait(barrier, len(greeted))

    def seq_push(item, pairs_of, whole):
        for k in range(1, n):
            j = (s + k) % n
            push_all(
                lambda j=j, k=k: (
                    pairs_of(j), whole, ref.seq_send.at[item, k], ref.seq_recv.at[item, k], {SEQ: j}
                )
            )

    def seq_wait(item, whole):
        for k in range(1, n):
            arrived(whole, ref.seq_recv.at[item, k])

    square = n == 4
    beside, across = s + 1 - 2 * (s % 2), (s + 2) % n

    def spread_first(item, buffer):
        mine = buffer.at[span(s, rows)]
        if not square:
            seq_push(item, lambda j: [(mine, mine)], mine)
            return
        for way, target in ((0, beside), (1, across)):
            push_all(
                lambda way=way, target=target: (
                    [(mine, mine)], mine, ref.seq_send.at[item, way], ref.seq_recv.at[item, way], {SEQ: target}
                )
            )

    def spread_second(item, buffer):
        if not square:
            return
        for way, source, target in ((0, beside, across), (1, across, beside)):
            arrived(buffer.at[span(source, rows)], ref.seq_recv.at[item, way])
            half = buffer.at[span(source, rows, rows // 2, way * (rows // 2))]
            push_all(
                lambda way=2 + way, target=target, half=half: (
                    [(half, half)], half, ref.seq_send.at[item, way], ref.seq_recv.at[item, way], {SEQ: target}
                )
            )

    def spread_wait(item, buffer):
        if not square:
            seq_wait(item, buffer.at[pl.ds(0, rows)])
            return
        for way in range(2):
            arrived(buffer.at[pl.ds(0, rows // 2)], ref.seq_recv.at[item, 2 + way])

    def chain_of(number, buffer, runs, count):
        def views(owner):
            return [buffer.at[span(run(owner), count)] for run in runs]

        whole = buffer.at[pl.ds(0, count * len(runs))]
        return types.SimpleNamespace(number=number, views=views, whole=whole)

    def piece_runs(first, last):
        return [lambda owner, j=j: j * m + owner for j in range(first, last)]

    def half_runs(half):
        return [lambda owner: owner * 2 + half]

    dense_in = chain_of(0, ref.dense_all, [lambda owner: owner], dense_rows)
    joint_a = chain_of(1, ref.joint_all, piece_runs(0, n // 2), piece)
    joint_b = chain_of(2, ref.joint_all, piece_runs(n // 2, n), piece)
    expand_a = chain_of(3, ref.expand_all, piece_runs(0, n // 2), piece)
    expand_b = chain_of(4, ref.expand_all, piece_runs(n // 2, n), piece)
    shrink_a = chain_of(5, ref.shrink_all, half_runs(0), shrink_rows // 2)
    shrink_b = chain_of(6, ref.shrink_all, half_runs(1), shrink_rows // 2)
    vector_in = chain_of(7, ref.vectors, [lambda owner: owner], n * VECTOR_ROWS)

    def gather_step(chain, hop):
        number = chain.number

        def views(owner):
            return [(view, view) for view in chain.views(owner() * CORES + c)]

        def swap(owner, when=None):
            push_all(
                lambda: (
                    views(owner),
                    chain.whole,
                    ref.swap_send.at[number, owner()],
                    ref.swap_recv.at[number, owner()],
                    twin,
                ),
                when,
            )

        def forward(side, owner, when):
            push_all(
                lambda: (
                    views(owner),
                    chain.whole,
                    ref.ag_send.at[number, side, hop],
                    ref.ag_recv.at[number, side, hop],
                    below if side else above,
                ),
                when,
            )

        if hop == 0:
            forward(0, lambda: z, lambda: z < line - 1)
            forward(1, lambda: z, lambda: z > 0)
            swap(lambda: z)
            return
        for side, owner, valid, more in (
            (0, lambda: (z - hop + line) % line, lambda: z >= hop, lambda: z < line - 1),
            (1, lambda: (z + hop) % line, lambda: z + hop < line, lambda: z > 0),
        ):
            pl.when(valid())(functools.partial(arrived, chain.whole, ref.ag_recv.at[number, side, hop - 1]))
            if hop < hops:
                forward(side, owner, lambda valid=valid, more=more: valid() & more())
            swap(owner, valid)

    def gather_wait(*chains):
        for chain in chains:
            for owner in range(line):
                arrived(chain.whole, ref.swap_recv.at[chain.number, owner])

    groups = (
        (vector_in, dense_in, joint_a, joint_b),
        (expand_a, expand_b),
        (shrink_a, shrink_b),
    )
    gather_queue = []
    for index, group in enumerate(groups):
        following = groups[index + 1] if index + 1 < len(groups) else ()
        for hop in range(1, hops + 1):
            for place, chain in enumerate(group):
                gather_queue.append((chain, hop))
                place -= len(group) - len(following)
                if hop == hops and 0 <= place:
                    gather_queue.append((following[place], 0))

    def gather(chain, hop):
        while gather_queue:
            entry = gather_queue.pop(0)
            gather_step(*entry)
            if entry[0] is chain and entry[1] == min(hop, hops):
                return

    def kind_of(first, total, core, chain, halves, count, columns):
        return types.SimpleNamespace(
            first=first, total=total, core=core, chain=chain, halves=halves, count=count, columns=columns
        )

    mid, low = mid_rows // 2, shrink_rows // 2
    dense_kind = kind_of(0, ref.dense_sum, ref.dense_core, ref.dense_chain, 1, dense_rows, width)
    joint_kind = kind_of(1, ref.joint_sum, ref.joint_core, ref.joint_chain, 2, mid, 3 * part)
    expand_kind = kind_of(3, ref.expand_sum, ref.expand_core, ref.expand_chain, 2, mid, hidden)
    shrink_kind = kind_of(5, ref.shrink_sum, ref.shrink_core, ref.shrink_chain, 2, low, width)
    adds, add_sem, sent = ref.adds, ref.add_sem, ref.sent
    rounds = types.SimpleNamespace(ring=0, pending=[None, None])

    def reduce_start(kind):
        for half in range(kind.halves):
            at = pl.ds(half * kind.count, kind.count)
            push_all(
                lambda at=at, half=half: (
                    [(kind.total.at[:, 1 - c, at], kind.core.at[:, at])],
                    kind.core.at[:, at],
                    ref.core_send.at[kind.first + half],
                    ref.core_recv.at[kind.first + half],
                    twin,
                )
            )

    def summed(slots, count, columns, into):
        @pl.loop(0, count // 16)
        def _(i):
            at = span(i, 16)
            total = adds[slots[0], at, 0:columns].astype(F32)
            for slot in slots[1:]:
                total = total + adds[slot, at, 0:columns].astype(F32)
            into(at, total)

    def added(sources, count, columns, into):
        copies = []
        for slot, source in enumerate(sources):
            copies.append(local(source, adds.at[slot, pl.ds(0, count), pl.ds(0, columns)], add_sem.at[slot]))
        for copy in copies:
            copy.wait()
        summed(range(len(sources)), count, columns, into)

    def add_slot(kind, slot):
        return adds.at[slot, pl.ds(0, kind.count), pl.ds(0, kind.columns)]

    def add_load(kind, source, slot):
        return pltpu.make_async_copy(source, add_slot(kind, slot), add_sem.at[slot])

    def blank(kind, slot):
        adds[slot, 0 : kind.count, 0 : kind.columns] = jnp.zeros((kind.count, kind.columns), BF)

    def reduce_round(kind, hop, side, valid):
        count, columns = kind.count, kind.columns
        ring = rounds.ring
        rounds.ring = 1 - ring
        if rounds.pending[ring] is not None:
            rounds.pending[ring]()
        target = lambda: (z + (line - hop) * (1 - 2 * side()) + line) % line
        joined = lambda: z + side() * (line - 1 - 2 * z) > 0
        device = lambda: {DP: d + CORES * (1 - 2 * side())}

        def at(half):
            return span(half, count)

        @pl.when(valid())
        def _():
            @pl.loop(0, kind.halves)
            def _(half):
                add_load(kind, kind.total.at[target(), c, at(half)], half * 3).start()
                add_load(kind, kind.core.at[target(), at(half)], half * 3 + 1).start()

            @pl.loop(0, kind.halves)
            def _(half):
                behind = kind.chain.at[side(), target(), at(half)]
                slots = [half * 3, half * 3 + 1]
                if hop > 1:
                    slots.append(half * 3 + 2)

                    @pl.when(joined())
                    def _():
                        arrived(behind, ref.rs_recv.at[kind.first + half, side(), hop - 2])
                        add_load(kind, behind, half * 3 + 2).start()

                    @pl.when(jnp.logical_not(joined()))
                    def _():
                        blank(kind, half * 3 + 2)

                add_load(kind, kind.total.at[target(), c, at(half)], half * 3).wait()
                add_load(kind, kind.core.at[target(), at(half)], half * 3 + 1).wait()
                if hop > 1:

                    @pl.when(joined())
                    def _():
                        add_load(kind, behind, half * 3 + 2).wait()

                def keep(where, total):
                    sent[ring * 2 + half, where, 0:columns] = total.astype(BF)

                summed(slots, count, columns, keep)
                remote(
                    sent.at[ring * 2 + half, pl.ds(0, count), pl.ds(0, columns)],
                    behind,
                    ref.rs_send.at[kind.first + half, side(), hop - 1],
                    ref.rs_recv.at[kind.first + half, side(), hop - 1],
                    device(),
                ).start()

        def settle():
            @pl.when(valid())
            def _():
                view = sent.at[0, pl.ds(0, count), pl.ds(0, columns)]
                for half in range(kind.halves):
                    remote(
                        view,
                        view,
                        ref.rs_send.at[kind.first + half, side(), hop - 1],
                        ref.rs_recv.at[kind.first + half, side(), hop - 1],
                        device(),
                    ).wait_send()

        rounds.pending[ring] = settle

    def reduce_hop(hop, *kinds):
        if hop > hops:
            return
        for kind in kinds:
            if hop == 1:
                for half in range(kind.halves):
                    arrived(
                        kind.core.at[:, pl.ds(half * kind.count, kind.count)], ref.core_recv.at[kind.first + half]
                    )
            if 2 * hop <= line:
                reduce_round(kind, hop, lambda: z * 2 // line, lambda: (z < hop) | (z >= line - hop))
            else:
                reduce_round(kind, hop, lambda: 0, lambda: z < hop)
                reduce_round(kind, hop, lambda: 1, lambda: z >= line - hop)

    def reduce_last(kind, half, into):
        at = span(half, kind.count)
        sources = [kind.total.at[z, c, at], kind.core.at[z, at], kind.chain.at[0, z, at], kind.chain.at[1, z, at]]
        for slot in range(2):
            add_load(kind, sources[slot], slot).start()
        for side, there in ((0, lambda: z > 0), (1, lambda: z < line - 1)):

            @pl.when(there())
            def _():
                arrived(sources[2 + side], ref.rs_recv.at[kind.first + half, side, hops - 1])
                add_load(kind, sources[2 + side], 2 + side).start()

            @pl.when(jnp.logical_not(there()))
            def _():
                blank(kind, 2 + side)

        for slot in range(2):
            add_load(kind, sources[slot], slot).wait()
        for side, there in ((0, lambda: z > 0), (1, lambda: z < line - 1)):
            pl.when(there())(lambda: add_load(kind, sources[2 + side], 2 + side).wait())

        def keep(where, total):
            into[where, 0 : kind.columns] = total

        summed(range(4), kind.count, kind.columns, keep)

    def finish_rows(kind, out):
        @pl.loop(0, kind.halves)
        def _(half):
            reduce_last(kind, half, ref.wide_one)
            view = ref.wide_one.at[pl.ds(0, kind.count), pl.ds(0, kind.columns)]
            local(view, out.at[span(half, kind.count)], add_sem.at[0]).wait()

    def finish_columns(kind, item, done, out, kinds):
        wide = kind.columns // kinds
        whole = done.at[pl.ds(0, piece)]
        each = kind.count // piece

        def pairs(j):
            return [
                (
                    done.at[span(j, piece), pl.ds(part_of * wide, wide)],
                    out.at[:, lanes(s, wide, part_of * wide * n)],
                )
                for part_of in range(kinds)
            ]

        def sems(j):
            k = (j - s + n) % n
            return ref.seq_send.at[item, k], ref.seq_recv.at[item, k], {SEQ: j}

        @pl.loop(0, kind.halves)
        def _(half):
            reduce_last(kind, half, ref.wide_one)
            view = ref.wide_one.at[pl.ds(0, kind.count), pl.ds(0, kind.columns)]
            local(view, done.at[span(half, kind.count)], add_sem.at[0]).wait()

            @pl.loop(0, each)
            def _(q):
                j = half * each + q

                @pl.when(j != s)
                def _():
                    for src, dst in pairs(j):
                        remote(src, dst, *sems(j)).start()

                @pl.when(j == s)
                def _():
                    copies = [
                        local(
                            ref.wide_one.at[span(q, piece), pl.ds(part_of * wide, wide)],
                            pairs(j)[part_of][1],
                            add_sem.at[part_of],
                        )
                        for part_of in range(kinds)
                    ]
                    for copy in copies:
                        copy.wait()

        for k in range(1, n):
            drains.append(lambda k=k: remote(whole, whole, *sems((s + k) % n)).wait_send())

    upstream, normed, qkv = ref.upstream, ref.normed, ref.qkv
    gate, mixed, grad_qkv = ref.gate, ref.mixed, ref.grad_qkv
    act, slope = ref.act, ref.slope
    left, right, dense = ref.left, ref.right, ref.dense
    wide_one, wide_two = ref.wide_one, ref.wide_two
    stage, gains, tables = ref.stage, ref.gains, ref.tables
    few = 32

    def joined_row(rows_of):
        lane = lax.broadcasted_iota(jnp.int32, (1, LANES), 1)
        value = ref.vectors[pl.ds(rows_of(0), 1), :]
        for q in range(1, LANES // piece):
            value = jnp.where(lane >= q * piece, ref.vectors[pl.ds(rows_of(q), 1), :], value)
        return value

    def vector_row(owner, row):
        return (owner % m * n + owner // m) * VECTOR_ROWS + row

    def unpack_vectors():
        group = LANES // piece
        for j in range(width // LANES):
            at = slice(j * LANES, (j + 1) * LANES)
            natural = lambda row: joined_row(lambda q: vector_row(j * group + q, row))
            for k in range(4):
                gains[k : k + 1, at] = natural(k)
            ref.offsets[0:1, at] = natural(7) + natural(8 + size.feed_pieces)
        for target, per, row, kinds, wide in (
            (ref.joint_bias, 3, 4, 3, part),
            (ref.expand_bias, size.feed_pieces, 8, 1, hidden),
        ):
            for j in range(kinds * wide // LANES):
                kind, inner = j // (wide // LANES), j % (wide // LANES)
                first = (kind * wide * n + inner * LANES) // piece + s * (wide // piece)
                target[0:1, j * LANES : (j + 1) * LANES] = joined_row(
                    lambda q: vector_row((first + q) // per, row + (first + q) % per)
                )

    def each_tile(body):
        def load(i, slot):
            return pltpu.make_async_copy(
                ref.tokens_all.at[span(i, rows)],
                stage.at[slot, pl.ds(0, rows), pl.ds(0, width)],
                ref.x_sem.at[slot],
            )

        load(0, 0).start()

        @pl.loop(0, n)
        def _(i):
            slot = i % 2
            load(i, slot).wait()

            @pl.when(i + 1 < n)
            def _():
                load(i + 1, 1 - slot).start()

            body(i, slot)

    def normal_of(slot, at):
        value = stage[slot, at, 0:width].astype(F32)
        center = value - jnp.mean(value, axis=-1, keepdims=True)
        spread = lax.rsqrt(jnp.mean(center * center, axis=-1, keepdims=True) + 1e-05)
        return center * spread, spread

    def norm_stage(which):
        def body(i, slot):
            @pl.loop(0, rows // few)
            def _(j):
                value, _ = normal_of(slot, span(j, few))
                value = value * gains[2 * which : 2 * which + 1, :] + gains[2 * which + 1 : 2 * which + 2, :]
                normed[pl.ds(pl.multiple_of(i * rows + j * few, few), few), :] = value.astype(BF)

        each_tile(body)

    def turn(value, at, sign):
        head = value[:, :LANES]
        lane = lax.broadcasted_iota(jnp.int32, head.shape, 1)
        lower = -sign * pltpu.roll(head, LANES - ROT // 2, 1)
        upper = sign * pltpu.roll(head, ROT // 2, 1)
        head = head * tables[0, at, :] + jnp.where(lane < ROT // 2, lower, upper) * tables[1, at, :]
        if value.shape[1] == LANES:
            return head
        return jnp.concatenate([head, value[:, LANES:]], axis=1)

    def joint_stage():
        @pl.loop(0, n)
        def _(i):
            at = span(i, rows)
            joint = nn(normed[at, :], right[0:width, 0 : 3 * part]) + ref.joint_bias[...]
            for kind in range(3):
                for head in range(heads):
                    first = kind * part + head * head_size
                    value = joint[:, first : first + head_size]
                    if kind < 2:
                        value = turn(value, at, 1.0)
                    qkv[at, first : first + head_size] = value.astype(BF)

    def gate_stage():
        @pl.loop(0, n)
        def _(i):
            gate[span(i, rows), :] = nt(upstream[span(i, rows), :], dense[...]).astype(BF)

    def attend_tile(head, i):
        keys = (i + 1) * rows
        at = pl.ds(i * rows, rows)
        seen = pl.ds(0, keys)
        q_at = pl.ds(head * head_size, head_size)
        k_at = pl.ds(part + head * head_size, head_size)
        v_at = pl.ds(2 * part + head * head_size, head_size)
        query = qkv[at, q_at]
        scores = nt(query, qkv[seen, k_at]) * scale
        row = lax.broadcasted_iota(jnp.int32, (rows, keys), 0) + i * rows
        column = lax.broadcasted_iota(jnp.int32, (rows, keys), 1)
        scores = jnp.where(column <= row, scores, -1e30)
        expo = jnp.exp(scores - jnp.max(scores, axis=-1, keepdims=True))
        probs = expo / jnp.sum(expo, axis=-1, keepdims=True)
        low_probs = probs.astype(BF)
        mixed[at, q_at] = nn(low_probs, qkv[seen, v_at]).astype(BF)
        back = gate[at, q_at]
        grad_probs = nt(back, qkv[seen, v_at])
        inner = jnp.sum(probs * grad_probs, axis=-1, keepdims=True)
        grad_scores = (probs * (grad_probs - inner)).astype(BF)
        grad_query = nn(grad_scores, qkv[seen, k_at]) * scale
        grad_qkv[at, q_at] = turn(grad_query, at, -1.0).astype(BF)
        for total, extra in ((wide_one, tn(grad_scores, query)), (wide_two, tn(low_probs, back))):
            for b in range(i + 1):
                here = (slice(0, rows), slice(b * head_size, (b + 1) * head_size))
                block = extra[b * rows : (b + 1) * rows]
                total[here] = block if i == n - 1 else total[here] + block

    def attend_stage(head):
        for i in range(n - 1, -1, -1):
            attend_tile(head, i)
        for b in range(n):
            at = pl.ds(b * rows, rows)
            here = (slice(0, rows), slice(b * head_size, (b + 1) * head_size))
            k_at = pl.ds(part + head * head_size, head_size)
            v_at = pl.ds(2 * part + head * head_size, head_size)
            grad_qkv[at, k_at] = turn(wide_one[here] * scale, at, -1.0).astype(BF)
            grad_qkv[at, v_at] = wide_two[here].astype(BF)

    def weight_grad(left_of, right_of, tiles, tall, columns, places):
        def stored(b, slot):
            return [
                pltpu.make_async_copy(
                    stage.at[slot, pl.ds(first, count), pl.ds(0, columns)], target, ref.stage_sem.at[slot]
                )
                for first, count, target in places(b)
            ]

        def settled(slot):
            view = stage.at[slot, pl.ds(0, tall), pl.ds(0, columns)]
            pltpu.make_async_copy(view, view, ref.stage_sem.at[slot]).wait()

        @pl.loop(0, tiles)
        def _(b):
            slot = b % 2

            @pl.when(b >= 2)
            def _():
                settled(slot)

            stage[slot, 0:tall, 0:columns] = tn(left_of(b), right_of()).astype(BF)
            for copy in stored(b, slot):
                copy.start()

        for b in range(max(tiles - 2, 0), tiles):
            settled(b % 2)

    def columns_of(buffer, count):
        return lambda b: buffer[:, lanes(b, count)]

    def block_places(out, count):
        return lambda b: [(0, count, out.at[b // CORES, b % CORES])]

    def piece_places(out, tall):
        def places(b):
            found = []
            for q in range(tall // piece):
                g = b * (tall // piece) + q
                owner = g % m
                found.append((q * piece, piece, out.at[owner // CORES, owner % CORES, span(g // m, piece)]))
            return found

        return places

    def dense_places(tall):
        def places(b):
            found = []
            for q in range(tall // dense_rows):
                owner = b * (tall // dense_rows) + q
                found.append((q * dense_rows, dense_rows, ref.dense_sum.at[owner // CORES, owner % CORES]))
            return found

        return places

    def expand_stage(start, stop):
        @pl.loop(start, stop)
        def _(i):
            wide_one[:, 0:hidden] = nn(normed[span(i, rows), :], left[...]) + ref.expand_bias[...]

            @pl.loop(0, rows // few)
            def _(j):
                value = wide_one[span(j, few), 0:hidden]
                share = 0.5 * (1.0 + lax.erf(value * 0.7071067811865476))
                density = jnp.exp(-0.5 * value * value) * 0.3989422804014327
                at = pl.ds(pl.multiple_of(i * rows + j * few, few), few)
                act[at, :] = (value * share).astype(BF)
                slope[at, :] = (share + value * density).astype(BF)

    def shrink_stage(start, stop):
        @pl.loop(start, stop)
        def _(i):
            wide_one[:, 0:hidden] = nt(upstream[span(i, rows), :], right[0:hidden, 0:width])

            @pl.loop(0, rows // few)
            def _(j):
                at = pl.ds(pl.multiple_of(i * rows + j * few, few), few)
                grad = (wide_one[span(j, few), 0:hidden] * slope[at, :].astype(F32)).astype(BF)
                slope[at, :] = grad
                ref.expand_total[...] += eights(grad.astype(F32))

    def owner_push(item, source, near, out, i):
        k = (i - s + n) % n
        mine = out.at[span(s, rows)]

        @pl.when(k != 0)
        def _():
            remote(source, mine, ref.seq_send.at[item, k], ref.seq_recv.at[item, k], {SEQ: i}).start()

        @pl.when(k == 0)
        def _():
            local(near, mine, add_sem.at[0]).wait()

    def owner_drain(item, buffer):
        whole = buffer.at[pl.ds(0, rows)]
        for k in range(1, n):
            drains.append(
                lambda k=k: remote(
                    whole, whole, ref.seq_send.at[item, k], ref.seq_recv.at[item, k], {SEQ: (s + k) % n}
                ).wait_send()
            )

    def output_stage():
        def tile_of(slot):
            return stage.at[slot, pl.ds(0, rows), pl.ds(0, width)]

        def moved(i, slot):
            return pltpu.make_async_copy(tile_of(slot), ref.output_part.at[span(i, rows)], ref.stage_sem.at[slot])

        @pl.loop(0, n)
        def _(i):
            at, slot = span(i, rows), i % 2
            wide_one[:, 0:width] = nn(mixed[at, :], dense[...])

            @pl.when(i >= 2)
            def _():
                moved(i - 2, slot).wait()
                owner_push(4, ref.output_part.at[span(i - 2, rows)], tile_of(slot), ref.output_all, i - 2)

            total = nn(act[at, :], right[0:hidden, 0:width]) + wide_one[:, 0:width]
            stage[slot, 0:rows, 0:width] = total.astype(BF)
            moved(i, slot).start()

        for i in range(max(n - 2, 0), n):
            moved(i, i % 2).wait()
            owner_push(4, ref.output_part.at[pl.ds(i * rows, rows)], tile_of(i % 2), ref.output_all, i)
        owner_drain(4, ref.output_part)

    def eights(value):
        return jnp.sum(value.reshape(value.shape[0] // 8, 8, value.shape[1]), axis=0)

    def input_stage(i, slot):
        at = span(i, rows)
        wide_one[:, 0:width] = nt(grad_qkv[at, :], right[0:width, 0 : 3 * part])
        wide_two[...] = nt(slope[at, :], left[...])

        @pl.loop(0, rows // few)
        def _(j):
            here = span(j, few)
            normal, _ = normal_of(slot, here)
            grad_one, grad_two = wide_one[here, 0:width], wide_two[here, :]
            total = grad_one * gains[0:1, :] + grad_two * gains[2:3, :]
            normed[pl.ds(pl.multiple_of(i * rows + j * few, few), few), :] = total.astype(BF)
            ref.gain_total[0] += eights(grad_one * normal)
            ref.gain_total[1] += eights(grad_one)
            ref.gain_total[2] += eights(grad_two * normal)
            ref.gain_total[3] += eights(grad_two)

        owner_push(5, normed.at[at], normed.at[at], ref.input_all, i)

    def joint_total_stage():
        ref.joint_total[...] = jnp.zeros_like(ref.joint_total)

        @pl.loop(0, length // few)
        def _(j):
            ref.joint_total[...] += eights(grad_qkv[span(j, few), :].astype(F32))

    small = ref.small
    wide_rows = size.gain_rows

    def small_pack():
        ref.own_total[...] = jnp.zeros_like(ref.own_total)

        @pl.loop(0, rows // few)
        def _(j):
            at = pl.ds(pl.multiple_of(s * rows + j * few, few), few)
            ref.own_total[...] += eights(upstream[at, :].astype(F32))

        small[0] = jnp.zeros_like(small[0])
        for first, source, count in (
            (0, ref.gain_total.at[0], wide_rows),
            (wide_rows, ref.gain_total.at[1], wide_rows),
            (2 * wide_rows, ref.gain_total.at[2], wide_rows),
            (3 * wide_rows, ref.gain_total.at[3], wide_rows),
            (4 * wide_rows, ref.own_total, wide_rows),
            (size.joint_small, ref.joint_total, 3 * part // LANES),
            (size.expand_small, ref.expand_total, hidden // LANES),
        ):
            for j in range(count):
                value = source[:, j * LANES : (j + 1) * LANES]
                small[0, first + j : first + j + 1, :] = jnp.sum(value, axis=0, keepdims=True)

    def small_core():
        push_all(
            lambda: (
                [(small.at[0], ref.small_in.at[0])], small.at[0], ref.small_send.at[0], ref.small_recv.at[0], twin
            )
        )

    def small_line():
        arrived(small.at[0], ref.small_recv.at[0])
        small[1] = small[0] + ref.small_in[0]
        for k in range(1, line):
            push_all(
                lambda k=k: (
                    [(small.at[1], ref.small_in.at[k])],
                    small.at[1],
                    ref.small_send.at[k],
                    ref.small_recv.at[k],
                    {DP: (z + k) % line * CORES + c},
                )
            )

    def small_seq():
        total = small[1]
        for k in range(1, line):
            arrived(small.at[0], ref.small_recv.at[k])
            total = total + ref.small_in[k]
        ref.small_all[s] = total
        mine = ref.small_all.at[s]
        seq_push(9, lambda j: [(mine, mine)], mine)

    def small_last():
        seq_wait(9, small.at[0])
        total = ref.small_all[0, 0 : 5 * wide_rows, :]
        for j in range(1, n):
            total = total + ref.small_all[j, 0 : 5 * wide_rows, :]
        ref.gain_grads[...] = total
        for j in range(n):
            ref.joint_grads[j] = ref.small_all[j, size.joint_small : size.expand_small, :]
            ref.expand_grads[j] = ref.small_all[j, size.expand_small : size.expand_small + hidden // LANES, :]

    def owner_sum(buffer):
        chunk = min(size.chunk, rows)
        for q in range(rows // chunk):
            for first in range(0, n, 4):
                sources = [buffer.at[pl.ds(j * rows + q * chunk, chunk)] for j in range(first, min(first + 4, n))]

                def into(where, total):
                    at = pl.ds(pl.multiple_of(where.start + q * chunk, 16), 16)
                    wide_one[at, 0:width] = total if first == 0 else wide_one[at, 0:width] + total

                added(sources, chunk, width, into)

    def own_tokens():
        return local(
            ref.tokens_all.at[span(s, rows)], stage.at[0, pl.ds(0, rows), pl.ds(0, width)], ref.x_sem.at[0]
        )

    def finish_output():
        copy = own_tokens()
        seq_wait(4, ref.output_all.at[pl.ds(0, rows)])
        owner_sum(ref.output_all)
        copy.wait()

        @pl.loop(0, rows // few)
        def _(j):
            at = span(j, few)
            total = stage[0, at, 0:width].astype(F32) + (wide_one[at, 0:width] + ref.offsets[...])
            stage[1, at, 0:width] = total.astype(BF)

        local(stage.at[1, pl.ds(0, rows), pl.ds(0, width)], ref.output, ref.stage_sem.at[0]).wait()

    def finish_input():
        copy = own_tokens()
        seq_wait(5, ref.input_all.at[pl.ds(0, rows)])
        owner_sum(ref.input_all)
        copy.wait()

        @pl.loop(0, rows // few)
        def _(j):
            at = span(j, few)
            normal, spread = normal_of(0, at)
            grad = wide_one[at, 0:width]
            through = grad - jnp.mean(grad, axis=-1, keepdims=True)
            through = through - normal * jnp.mean(grad * normal, axis=-1, keepdims=True)
            own = upstream[pl.ds(pl.multiple_of(s * rows + j * few, few), few), :].astype(F32)
            wide_two[at, :] = own + spread * through

        local(wide_two, ref.grad_tokens, ref.stage_sem.at[0]).wait()

    def load_joint():
        return local(ref.joint_all, right.at[pl.ds(0, width), pl.ds(0, 3 * part)], ref.load_sem.at[0])

    def joint_pairs(j):
        return [
            (
                ref.joint_own.at[:, lanes(j, part, kind * width)],
                ref.joint_all.at[span(s * m + d, piece), pl.ds(kind * part, part)],
            )
            for kind in range(3)
        ]

    def expand_pairs(j):
        return [(ref.expand_own.at[:, lanes(j, hidden)], ref.expand_all.at[span(s * m + d, piece)])]

    def vector_pairs(j):
        return [(ref.vector_own, ref.vectors.at[span(d * n + s, VECTOR_ROWS)])]

    seq_push(0, joint_pairs, ref.joint_all.at[pl.ds(0, piece)])
    seq_push(8, vector_pairs, ref.vector_own)

    def room(buffer, slot, source):
        return buffer.at[slot, pl.ds(0, source.shape[0]), pl.ds(0, source.shape[1])]

    joint_held = ref.adds.at[0, pl.ds(0, piece), pl.ds(0, 3 * part)]
    moves = [
        ([(ref.dense_own, room(ref.sent, 0, ref.dense_own))], ref.dense_all.at[span(d, dense_rows)]),
        (
            [
                (src, ref.adds.at[0, pl.ds(0, piece), pl.ds(kind * part, part)])
                for kind, (src, _) in enumerate(joint_pairs(s))
            ],
            ref.joint_all.at[span(s * m + d, piece)],
        ),
        ([(ref.tokens, room(stage, 0, ref.tokens))], ref.tokens_all.at[span(s, rows)]),
        ([(expand_pairs(s)[0][0], ref.adds.at[1, pl.ds(0, piece), pl.ds(0, hidden)])], expand_pairs(s)[0][1]),
        ([(ref.shrink_own, room(stage, 1, ref.shrink_own))], ref.shrink_all.at[span(d, shrink_rows)]),
    ]
    held = [moves[0][0][0][1], joint_held, moves[2][0][0][1], moves[3][0][0][1], moves[4][0][0][1]]
    fetched = [
        [local(src, dst, ref.own_sem.at[k, q]) for q, (src, dst) in enumerate(pairs)]
        for k, (pairs, _) in enumerate(moves)
    ]
    own_vectors = [local(src, dst, ref.own_sem.at[5, 0]) for src, dst in vector_pairs(s)]
    own_upstream = local(ref.cotangent, upstream.at[span(s, rows)], ref.own_sem.at[5, 1])
    stored = []
    for k, copies in enumerate(fetched):
        for copy in copies:
            copy.wait()
        stored.append(local(held[k], moves[k][1], ref.own_sem.at[k, 0]))
    stored[0].wait()
    gather_step(dense_in, 0)
    stored[2].wait()
    spread_first(2, ref.tokens_all)
    own_vectors[0].wait()
    seq_wait(8, ref.vector_own)
    gather_step(vector_in, 0)
    stored[1].wait()
    seq_wait(0, ref.joint_all.at[pl.ds(0, piece)])
    gather_step(joint_a, 0)
    gather_step(joint_b, 0)
    seq_push(1, expand_pairs, ref.expand_all.at[pl.ds(0, piece)])
    ref.gain_total[...] = jnp.zeros_like(ref.gain_total)
    ref.expand_total[...] = jnp.zeros_like(ref.expand_total)
    stored[3].wait()
    stored[4].wait()
    own_upstream.wait()
    gather(joint_b, 1)
    gather(dense_in, 2)
    spread_second(2, ref.tokens_all)
    spread_first(3, upstream)
    gather(joint_b, 2)
    gather(vector_in, hops)
    gather_wait(vector_in)
    unpack_vectors()
    seq_wait(1, ref.expand_all.at[pl.ds(0, piece)])
    spread_wait(2, ref.tokens_all)
    gather(dense_in, hops)
    norm_stage(0)
    gather(expand_a, 0)
    spread_second(3, upstream)
    gather(expand_b, 0)
    gather_wait(dense_in, joint_a, joint_b)
    copy_one = load_joint()
    copy_two = local(ref.dense_all, dense, ref.load_sem.at[1])
    copy_one.wait()
    joint_stage()
    gather(expand_a, 1)
    spread_wait(3, upstream)
    copy_two.wait()
    gate_stage()
    gather(expand_b, 1)
    for head in range(heads):
        attend_stage(head)
    tall = min(part, size.high)
    weight_grad(columns_of(mixed, tall), lambda: upstream[...], part // tall, tall, width, dense_places(tall))
    reduce_start(dense_kind)
    gather(expand_a, 2)
    weight_grad(
        columns_of(normed, mid_rows),
        lambda: grad_qkv[...],
        m,
        mid_rows,
        3 * part,
        piece_places(ref.joint_sum, mid_rows),
    )
    reduce_start(joint_kind)
    gather(expand_b, 2)
    joint_total_stage()
    norm_stage(1)
    reduce_hop(1, dense_kind, joint_kind)
    gather(shrink_a, 0)
    reduce_hop(2, dense_kind)
    gather(shrink_b, 0)
    gather_wait(expand_a, expand_b)
    copy_one = local(ref.expand_all, left, ref.load_sem.at[0])
    reduce_hop(2, joint_kind)
    copy_one.wait()
    expand_stage(0, n // 2)
    gather(shrink_a, 1)
    expand_stage(n // 2, n)
    gather(shrink_b, 1)
    reduce_hop(3, dense_kind, joint_kind)
    weight_grad(
        columns_of(act, shrink_rows),
        lambda: upstream[...],
        m,
        shrink_rows,
        width,
        block_places(ref.shrink_sum, shrink_rows),
    )
    reduce_start(shrink_kind)
    gather(shrink_a, 2)
    for hop in range(4, hops + 1):
        reduce_hop(hop, dense_kind, joint_kind)
    reduce_hop(1, shrink_kind)
    gather(shrink_b, 2)
    finish_rows(dense_kind, ref.dense_grad)
    finish_columns(joint_kind, 6, ref.joint_done, ref.joint_grad, 3)
    gather(shrink_b, hops)
    gather_wait(shrink_a, shrink_b)
    local(ref.shrink_all, right.at[pl.ds(0, hidden), pl.ds(0, width)], ref.load_sem.at[0]).wait()
    shrink_stage(0, n)
    reduce_hop(2, shrink_kind)
    weight_grad(
        columns_of(normed, mid_rows),
        lambda: slope[...],
        m,
        mid_rows,
        hidden,
        piece_places(ref.expand_sum, mid_rows),
    )
    reduce_start(expand_kind)
    for hop in range(3, hops + 1):
        reduce_hop(hop, shrink_kind)
    reduce_hop(1, expand_kind)
    output_stage()
    copy_one = load_joint()
    reduce_hop(2, expand_kind)
    copy_one.wait()
    each_tile(input_stage)
    owner_drain(5, ref.input_all)
    small_pack()
    small_core()
    for hop in range(3, hops + 1):
        reduce_hop(hop, expand_kind)
    small_line()
    finish_rows(shrink_kind, ref.shrink_grad)
    small_seq()
    finish_output()
    finish_columns(expand_kind, 7, ref.expand_done, ref.expand_grad, 1)
    small_last()
    finish_input()
    seq_wait(6, ref.joint_done.at[pl.ds(0, piece)])
    seq_wait(7, ref.expand_done.at[pl.ds(0, piece)])
    for pending in rounds.pending:
        if pending is not None:
            pending()
    for drain in drains:
        drain()


def run_kernel(size, inputs):
    n, m, line, hops = size.n, size.m, size.line, size.hops
    rows, width, piece, part, hidden = size.rows, size.width, size.piece, size.part, size.hidden
    dense_rows, mid_rows, shrink_rows, length = size.dense_rows, size.mid_rows, size.shrink_rows, size.length
    anywhere, vmem = pl.BlockSpec(memory_space=pl.ANY), pl.BlockSpec(memory_space=pltpu.VMEM)

    def reduced(count, columns):
        shape = (count, columns)
        return ((line, CORES) + shape, BF), ((line,) + shape, BF), ((2, line) + shape, BF)

    dense, joint = reduced(dense_rows, width), reduced(mid_rows, 3 * part)
    expand, shrink = reduced(mid_rows, hidden), reduced(shrink_rows, width)
    small_outputs = dict(
        gain_grads=((5 * size.gain_rows, LANES), F32),
        joint_grads=((n, 3 * part // LANES, LANES), F32),
        expand_grads=((n, hidden // LANES, LANES), F32),
    )
    outputs = dict(
        output=((rows, width), BF),
        grad_tokens=((rows, width), F32),
        dense_grad=((dense_rows, width), F32),
        shrink_grad=((shrink_rows, width), F32),
        joint_grad=((piece, 3 * width), F32),
        expand_grad=((piece, n * hidden), F32),
        dense_all=((part, width), BF),
        joint_all=((width, 3 * part), BF),
        expand_all=((width, hidden), BF),
        shrink_all=((hidden, width), BF),
        tokens_all=((length, width), BF),
        output_all=((length, width), BF),
        input_all=((length, width), BF),
        output_part=((length, width), BF),
        joint_done=((mid_rows, 3 * part), F32),
        expand_done=((mid_rows, hidden), F32),
        dense_sum=dense[0],
        dense_core=dense[1],
        dense_chain=dense[2],
        joint_sum=joint[0],
        joint_core=joint[1],
        joint_chain=joint[2],
        expand_sum=expand[0],
        expand_core=expand[1],
        expand_chain=expand[2],
        shrink_sum=shrink[0],
        shrink_core=shrink[1],
        shrink_chain=shrink[2],
    )
    dma = pltpu.SemaphoreType.DMA
    small = (size.small, LANES)
    scratch = dict(
        upstream=pltpu.VMEM((length, width), BF),
        normed=pltpu.VMEM((length, width), BF),
        qkv=pltpu.VMEM((length, 3 * part), BF),
        gate=pltpu.VMEM((length, part), BF),
        mixed=pltpu.VMEM((length, part), BF),
        grad_qkv=pltpu.VMEM((length, 3 * part), BF),
        act=pltpu.VMEM((length, hidden), BF),
        slope=pltpu.VMEM((length, hidden), BF),
        left=pltpu.VMEM((width, hidden), BF),
        right=pltpu.VMEM((max(width, hidden), max(width, 3 * part)), BF),
        dense=pltpu.VMEM((part, width), BF),
        wide_one=pltpu.VMEM((max(rows, size.chunk), max(width, hidden)), F32),
        wide_two=pltpu.VMEM((rows, width), F32),
        stage=pltpu.VMEM((2, size.high, size.broad), BF),
        adds=pltpu.VMEM((6, size.chunk, size.broad), BF),
        sent=pltpu.VMEM((4, size.chunk, size.broad), BF),
        vectors=pltpu.VMEM((n * m * VECTOR_ROWS, LANES), F32),
        gains=pltpu.VMEM((4, width), F32),
        offsets=pltpu.VMEM((1, width), F32),
        joint_bias=pltpu.VMEM((1, 3 * part), F32),
        expand_bias=pltpu.VMEM((1, hidden), F32),
        gain_total=pltpu.VMEM((4, 8, width), F32),
        own_total=pltpu.VMEM((8, width), F32),
        joint_total=pltpu.VMEM((8, 3 * part), F32),
        expand_total=pltpu.VMEM((8, hidden), F32),
        small=pltpu.VMEM((2,) + small, F32),
        small_in=pltpu.VMEM((line,) + small, F32),
        small_all=pltpu.VMEM((n,) + small, F32),
        seq_send=dma((10, max(n, 4))),
        seq_recv=dma((10, max(n, 4))),
        ag_send=dma((8, 2, hops)),
        ag_recv=dma((8, 2, hops)),
        swap_send=dma((8, line)),
        swap_recv=dma((8, line)),
        core_send=dma((7,)),
        core_recv=dma((7,)),
        rs_send=dma((7, 2, hops)),
        rs_recv=dma((7, 2, hops)),
        small_send=dma((line,)),
        small_recv=dma((line,)),
        add_sem=dma((6,)),
        stage_sem=dma((2,)),
        load_sem=dma((2,)),
        own_sem=dma((6, 3)),
        x_sem=dma((2,)),
    )
    names = list(inputs) + list(outputs) + list(small_outputs) + list(scratch)
    results = pl.pallas_call(
        functools.partial(kernel, size, names),
        out_shape=[
            jax.ShapeDtypeStruct(shape, kind)
            for shape, kind in list(outputs.values()) + list(small_outputs.values())
        ],
        in_specs=[vmem if name == next(reversed(inputs)) else anywhere for name in inputs],
        out_specs=[anywhere] * len(outputs) + [vmem] * len(small_outputs),
        scratch_shapes=list(scratch.values()),
        compiler_params=pltpu.CompilerParams(
            collective_id=0, has_side_effects=True, vmem_limit_bytes=64 * 2**20 - 2**17
        ),
        name="block",
    )(*inputs.values())
    return types.SimpleNamespace(**dict(zip(list(outputs) + list(small_outputs), results)))


def block_plan(n, m, tokens, cotangent, shards):
    (
        first_gain,
        first_shift,
        second_gain,
        second_shift,
        joint_weight,
        joint_bias,
        dense_weight,
        dense_bias,
        expand_weight,
        expand_bias,
        shrink_weight,
        shrink_bias,
    ) = shards
    rows, width = tokens.shape[1:]
    size = sizes_of(n, m, rows, width, expand_weight.shape[1])
    piece, devices = size.piece, n * m
    vectors = jnp.concatenate(
        [
            first_gain,
            first_shift,
            second_gain,
            second_shift,
            joint_bias,
            dense_bias,
            expand_bias,
            shrink_bias,
        ]
    )
    vectors = vectors.astype(F32).reshape(-1, 1, piece)
    vectors = jnp.broadcast_to(vectors, (vectors.shape[0], LANES // piece, piece)).reshape(-1, LANES)
    vectors = jnp.pad(vectors, ((0, VECTOR_ROWS - vectors.shape[0]), (0, 0)))
    got = run_kernel(
        size,
        dict(
            tokens=tokens[0],
            cotangent=cotangent[0],
            joint_own=joint_weight,
            expand_own=expand_weight,
            dense_own=dense_weight,
            shrink_own=shrink_weight,
            vector_own=vectors,
            tables=turn_tables(size.length),
        ),
    )
    index = lax.axis_index(SEQ) * m + lax.axis_index(DP)

    def own(values):
        return lax.dynamic_index_in_dim(values.reshape(devices, -1), index, 0, keepdims=False)

    gains = lax.dynamic_slice_in_dim(got.gain_grads.reshape(5, width), index * piece, piece, 1)
    joint_grads = jnp.swapaxes(got.joint_grads.reshape(n, 3, size.part), 0, 1)
    return (
        got.output[None],
        got.grad_tokens[None],
        gains[0],
        gains[1],
        gains[2],
        gains[3],
        got.joint_grad,
        own(joint_grads),
        got.dense_grad,
        gains[4],
        got.expand_grad,
        own(got.expand_grads),
        got.shrink_grad,
        gains[4],
    )


def solution(mesh):
    n, m = mesh.shape[SEQ], mesh.shape[DP]

    def body(tokens, cotangent, *shards):
        return block_plan(n, m, tokens, cotangent, shards)

    both = (SEQ, DP)
    tokens = P(DP, SEQ, None)
    vector, matrix = P(both), P(both, None)
    return jax.shard_map(
        body,
        mesh=mesh,
        in_specs=(tokens, tokens) + (vector,) * 4 + (matrix, vector) * 4,
        out_specs=(tokens, tokens) + (vector,) * 4 + (matrix, vector) * 4,
        check_vma=False,
    )
```

time: 1100 us -> 470 us (0.43)
  Pallas kernels: 0 us -> 443 us
  waiting for transfers between devices: 409 us -> 0 us
  matrix products: 169 us -> 0 us
  starting transfers between devices: 167 us -> 0 us
  local copies, waits for them, and re-layouts: 173 us -> 21.3 us
  other arithmetic: 112 us -> 3.33 us
  blocking collectives: 43.7 us -> 0 us
  between operations: 16.9 us -> 0.71 us
    pallas_call x0 -> x1, Pallas kernels: none -> 443 us  [run_kernel(): pl.pallas_call(functools.partial(kernel, size, names), out_shape=[jax.Sha...]
    ppermute x80 -> x0, waiting for transfers between devices: 284 us -> none  [the longest x12 88.2 us: gather_dp(): downs.append(lax.ppermute(downs[-1], 'dp', self.down))]
    ppermute x80 -> x0, starting transfers between devices: 167 us -> none  [the longest x12 56.5 us: scatter_dp(): rising = lax.ppermute(first, 'dp', self.up)]
    dot_general x17 -> x0, matrix products: 160 us -> none  [the longest x4 64.4 us: mm_last(): lax.dot_general(left, right, (((1,), (1,)), ((), ())), preferred_element_...]
    unnamed x2 -> x0, waiting for transfers between devices: 125 us -> none
    convert_element_type x25 -> x0, other arithmetic: 53.8 us -> none  [the longest x4 13.7 us: scatter_dp(): held = (self.pick(parts, self.c).astype(F32) + sent.astype(F32)).astype(BF)]
    unnamed x1 -> x0, blocking collectives: 43.7 us -> none
    unnamed x233 -> x17, local copies, waits for them, and re-layouts: 46.7 us -> 10.7 us
  transfers between devices with their start and end apart: 81 -> 0, of which waited for: 29 -> 0; matrix products, arithmetic and copies ran while one was open for 40% -> 0% of each run, Pallas kernels for 0% -> 0%
where the time goes in v3:
time: 470 us; the launch traced here: 468 us
  Pallas kernels  443 us (94%)
  local copies, waits for them, and re-layouts  21.3 us (5%)
    pallas_call x1, Pallas kernels, run_kernel(): pl.pallas_call(functools.partial(kernel, size, names), out_shape=[jax.Sha...  443 us
    unnamed x17, local copies, waits for them, and re-layouts  10.7 us

profile of v3, /device:TPU:0, one launch (start us, length us, event | category | flops | bytes accessed | tf_op | source)
XLA Modules:
  0.0 468.3 jit_solution(7620433673758692843)
XLA Ops:
  0.6 5.4 %concatenate.9 = bf16[832]{0:T(1024)(128)(2,1)S(1)} concatenate(bf16[64]{0:T(256)(128)(2,1)} %param.16, bf16[64]{0:T(256)(128)(2,1)} %param.17, bf16[64]{0:T(256)(128)(2,1)} %param.18, bf16[64]{0:T(256)(128)(2,1)} %param.19, bf16[192]{0:T(256)(128)(2,1)} %param.21, bf16[64]{0:T(256)(128)(2,1)} %param.23, bf16[256]{0:T(256)(128)(2,1)} %param.25, bf16[64]{0:T(256)(128)(2,1)} %param.27), dimensions={0} | concatenate | bytes 3328 | tf_op jit(solution)/shard_map/concatenate | solution.py:1212
  6.1 0.1 reshape.63
  6.1 0.1 reshape.58
  6.2 0.6 pad.4.refs_6_
  6.8 1.9 fusion.1
  8.8 0.1 pad.12.clone
  8.9 0.1 pad.9.clone
  9.0 0.3 maximum_bitcast_fusion
  9.3 1.0 pad_maximum_fusion.refs_7_
  10.3 443.0 %block.1 = (bf16[256,2048]{1,0:T(8,128)(2,1)}, f32[256,2048]{1,0:T(8,128)}, f32[64,2048]{1,0:T(8,128)}, f32[256,2048]{1,0:T(8,128)}, f32[64,6144]{1,0:T(8,128)},...) custom-call(bf16[256,2048]{1,0:T(8,128)(2,1)} %bitcast.23, ...), custom_call_target="tpu_custom_call" | custom-call | tf_op jit(solution)/shard_map/block/pallas_call | solution.py:1177
  453.3 0.9 reshape.59
  454.3 0.5 slice_bitcast_fusion
  454.8 0.8 reshape.60
  455.6 0.1 reshape.61
  455.7 0.6 constant_dynamic-slice_fusion.1
  456.3 0.8 reshape.62
  457.0 0.6 constant_dynamic-slice_fusion
  457.6 0.5 copy.36
  458.1 2.3 copy.37
  460.4 3.3 copy.38
  463.7 1.1 copy.39
  464.9 0.8 copy.40
  465.7 1.3 copy.41
  467.0 1.3 copy.42
  (16 shorter events, 0.1 us)
Async XLA Ops:
  453.3 10.4 %copy-start.2 = (f32[64,6144]{1,0:T(8,128)S(1)}, f32[64,6144]{1,0:T(8,128)}, u32[]{:S(2)}) copy-start(f32[64,6144]{1,0:T(8,128)} %get-tuple-element.89) | copy-start | bytes 4718596
  454.8 10.1 %copy-start.4 = (f32[64]{0:T(128)}, f32[64]{0:T(128)S(1)}, u32[]{:S(2)}) copy-start(f32[64]{0:T(128)S(1)} %get-tuple-element.92) | copy-start | bytes 772
  460.4 4.4 copy-start.3
  460.4 5.2 %copy-start.1 = (f32[64,8192]{1,0:T(8,128)S(1)}, f32[64,8192]{1,0:T(8,128)}, u32[]{:S(2)}) copy-start(f32[64,8192]{1,0:T(8,128)} %get-tuple-element.93) | copy-start | bytes 6291460
  463.7 3.3 copy-start
